TPU v7x, 32 devices: a whole 2x2x4 slice. The times are simulated.
32 devices in a mesh: dp: 8 (over z, y), seq: 4 (over x, core).
Axes of the slice: x: 2, y: 2, z: 4, core: 2. Of those that a mesh axis runs over, the one named last changes fastest.
Arguments:
- hidden_states: bfloat16 [64, 512, 768], P('dp', 'seq'), may hold values from -6 to 6
- prev_logits: bfloat16 [64, 12, 512, 512], P('dp', None, 'seq'), may hold values from -6 to 6
- lengths: int32 [64], P('dp'), may hold values from 128 to 512, as said below
- w_qkv: bfloat16 [768, 2304], P('dp', 'seq'), may hold values from -0.21875 to 0.21875
- w_out: bfloat16 [768, 768], P('dp', 'seq'), may hold values from -0.875 to 0.875
- w_in: bfloat16 [768, 3072], P('dp', 'seq'), may hold values from -0.21875 to 0.21875
- w_down: bfloat16 [3072, 768], P('dp', 'seq'), may hold values from -0.109375 to 0.109375
- b_in: bfloat16 [3072], P(('dp', 'seq')), may hold values from -3 to 3
- vectors: bfloat16 [8, 768], P('seq', 'dp')
- cotangent: bfloat16 [64, 512, 768], P('dp', 'seq'), may hold values from -6 to 6
Outputs:
- hidden_out: bfloat16 [64, 512, 768], P('dp', 'seq')
- grad_hidden: bfloat16 [64, 512, 768], P('dp', 'seq')
- grad_logits: bfloat16 [64, 12, 512, 512], P('dp', None, 'seq')
- grad_w_qkv: float32 [768, 2304], P('dp', 'seq')
- grad_w_out: float32 [768, 768], P('dp', 'seq')
- grad_w_in: float32 [768, 3072], P('dp', 'seq')
- grad_w_down: float32 [3072, 768], P('dp', 'seq')
- grad_b_in: float32 [3072], P(('dp', 'seq'))
- grad_vectors: float32 [8, 768], P('seq', 'dp')
Inputs may be any that keep to these rules, and one draw needn't show every extreme that they name: `lengths`: keys at positions from a sequence's length on are padding. Among the 8 sequences of each index of dp, at least one is full.
All inputs are finite; a program needn't handle non-finite values.
Results may differ from a plain program's by a relative error of at most 0.017.
Values may be sent and summed in bfloat16 or wider, within the bound.
No kernel may reach another device: no remote copies, remote signals or barrier semaphores. Data moves between devices by JAX's collectives and lax.ppermute only.
A program may use at most 256 MiB of HBM per device.

v0:
```python
import math

import jax
import jax.numpy as jnp
from jax import lax
from jax.sharding import PartitionSpec as P

D = 768
HEADS = 12
HEAD_DIM = 64


def gelu_exact(values):
    return jax.nn.gelu(values, approximate=False)


def gather_weights(w_qkv, w_out, w_in, w_down, b_in, vectors):
    inner_part = (
        lax.all_gather(w_qkv, "seq", axis=1, tiled=True),
        lax.all_gather(w_out, "seq", axis=1, tiled=True),
        lax.all_gather(w_in, "seq", axis=1, tiled=True),
        lax.all_gather(w_down, "seq", axis=1, tiled=True),
        lax.all_gather(b_in.reshape(1, -1), "seq", axis=1, tiled=True),
        lax.all_gather(vectors, "seq", axis=0, tiled=True),
    )
    whole = (
        lax.all_gather(inner_part[0], "dp", axis=0, tiled=True),
        lax.all_gather(inner_part[1], "dp", axis=0, tiled=True),
        lax.all_gather(inner_part[2], "dp", axis=0, tiled=True),
        lax.all_gather(inner_part[3], "dp", axis=0, tiled=True),
        lax.all_gather(inner_part[4], "dp", axis=0, tiled=True),
        lax.all_gather(inner_part[5], "dp", axis=1, tiled=True),
    )
    return (whole[0], whole[1], whole[2], whole[3], whole[4].reshape(-1), whole[5])


def layer_norm(values, gain, shift):
    average = jnp.mean(values, -1, keepdims=True)
    centred = values - average
    spread = jnp.mean(centred * centred, -1, keepdims=True)
    inverse = lax.rsqrt(spread + 1e-06)
    normed = centred * inverse
    return (normed * gain + shift, normed, inverse)


def norm_back(grad_normed, normed, inverse):
    first_mean = jnp.mean(grad_normed, -1, keepdims=True)
    second_mean = jnp.mean(grad_normed * normed, -1, keepdims=True)
    return inverse * (grad_normed - first_mean - normed * second_mean)


def scores(query_blk, key_blk, prev_blk, len_blk):
    count, rows = (query_blk.shape[0], query_blk.shape[1])
    total = key_blk.shape[1]
    query_heads = query_blk.reshape(count, rows, HEADS, HEAD_DIM)
    key_heads = key_blk.reshape(count, total, HEADS, HEAD_DIM)
    raw = jnp.einsum(
        "brhd,bkhd->bhrk", query_heads, key_heads, preferred_element_type=jnp.float32
    ) * HEAD_DIM ** (-0.5)
    raw = raw + prev_blk.astype(jnp.float32)
    valid = jnp.arange(total, dtype=jnp.int32)[None, :] < len_blk[:, None]
    return jnp.where(valid[:, None, None, :], raw, -1000000000.0)


def attend(block_item):
    query_blk, kv_blk, prev_blk, len_blk = block_item
    count, rows = (query_blk.shape[0], query_blk.shape[1])
    total = kv_blk.shape[1]
    raw = scores(query_blk, kv_blk[..., :D], prev_blk, len_blk)
    largest = jnp.max(raw, -1, keepdims=True)
    expo = jnp.exp(raw - largest)
    summed = jnp.sum(expo, -1, keepdims=True)
    probs = expo / summed
    log_total = largest[..., 0] + jnp.log(summed[..., 0])
    value_heads = kv_blk[..., D:].reshape(count, total, HEADS, HEAD_DIM)
    mixed = jnp.einsum(
        "bhrk,bkhd->brhd",
        probs.astype(jnp.bfloat16),
        value_heads,
        preferred_element_type=jnp.float32,
    )
    return (mixed.reshape(count, rows, D).astype(jnp.bfloat16), log_total)


def attend_back(block_item):
    query_blk, kv_blk, prev_blk, len_blk, total_blk, grad_ctx = block_item
    count, rows = (query_blk.shape[0], query_blk.shape[1])
    total = kv_blk.shape[1]
    scale = HEAD_DIM ** (-0.5)
    raw = scores(query_blk, kv_blk[..., :D], prev_blk, len_blk)
    probs = jnp.exp(raw - total_blk[..., None])
    query_heads = query_blk.reshape(count, rows, HEADS, HEAD_DIM)
    key_heads = kv_blk[..., :D].reshape(count, total, HEADS, HEAD_DIM)
    value_heads = kv_blk[..., D:].reshape(count, total, HEADS, HEAD_DIM)
    grad_heads = grad_ctx.reshape(count, rows, HEADS, HEAD_DIM)
    grad_probs = jnp.einsum(
        "brhd,bkhd->bhrk", grad_heads, value_heads, preferred_element_type=jnp.float32
    )
    weighted = jnp.sum(probs * grad_probs, -1, keepdims=True)
    grad_scores = (probs * (grad_probs - weighted)).astype(jnp.bfloat16)
    grad_query = (
        jnp.einsum("bhrk,bkhd->brhd", grad_scores, key_heads, preferred_element_type=jnp.float32)
        * scale
    )
    grad_key = (
        jnp.einsum("bhrk,brhd->bkhd", grad_scores, query_heads, preferred_element_type=jnp.float32)
        * scale
    )
    grad_value = jnp.einsum(
        "bhrk,brhd->bkhd",
        probs.astype(jnp.bfloat16),
        grad_heads,
        preferred_element_type=jnp.float32,
    )
    grad_kv = jnp.concatenate(
        [grad_key.reshape(count, total, D), grad_value.reshape(count, total, D)], -1
    )
    return (grad_query.reshape(count, rows, D).astype(jnp.bfloat16), grad_kv, grad_scores)


def block_sizes(seq_count, rows):
    per_block = math.gcd(seq_count, max(1, 512 // rows))
    return (per_block, seq_count // per_block)


def forward(weights, hidden_states, prev_logits, lengths):
    w_qkv, w_out, w_in, w_down, b_in, vectors = weights
    seq_count, rows, width = hidden_states.shape
    per_block, blocks = block_sizes(seq_count, rows)
    vec_rows = vectors.astype(jnp.float32)
    tok_rows = hidden_states.reshape(seq_count * rows, width)
    qkv = jnp.dot(tok_rows, w_qkv, preferred_element_type=jnp.float32)
    queries = (qkv[:, :D] + vec_rows[0]).astype(jnp.bfloat16)
    key_rows = qkv[:, D : 2 * D].astype(jnp.bfloat16)
    value_rows = (qkv[:, 2 * D :] + vec_rows[1]).astype(jnp.bfloat16)
    local_kv = jnp.concatenate([key_rows, value_rows], 1).reshape(seq_count, rows, 2 * D)
    all_kv = lax.all_gather(local_kv, "seq", axis=1, tiled=True)
    total = all_kv.shape[1]
    context, log_total = lax.map(
        attend,
        (
            queries.reshape(blocks, per_block, rows, D),
            all_kv.reshape(blocks, per_block, total, 2 * D),
            prev_logits.reshape(blocks, per_block, HEADS, rows, total),
            lengths.reshape(blocks, per_block),
        ),
    )
    context = context.reshape(seq_count * rows, D)
    attn_out = jnp.dot(context, w_out, preferred_element_type=jnp.float32) + vec_rows[2]
    first, normed_one, inverse_one = layer_norm(
        tok_rows.astype(jnp.float32) + attn_out, vec_rows[3], vec_rows[4]
    )
    first_low = first.astype(jnp.bfloat16)
    inner = jnp.dot(first_low, w_in, preferred_element_type=jnp.float32) + b_in.astype(jnp.float32)
    gelu_out = gelu_exact(inner).astype(jnp.bfloat16)
    branch = jnp.dot(gelu_out, w_down, preferred_element_type=jnp.float32) + vec_rows[5]
    second, normed_two, inverse_two = layer_norm(first + branch, vec_rows[6], vec_rows[7])
    saved = (
        tok_rows,
        queries,
        all_kv,
        log_total,
        context,
        normed_one,
        inverse_one,
        first_low,
        inner,
        gelu_out,
        normed_two,
        inverse_two,
    )
    return (second, saved)


def backward(weights, saved, prev_logits, lengths, cotangent):
    w_qkv, w_out, w_in, w_down, b_in, vectors = weights
    (
        tok_rows,
        queries,
        all_kv,
        log_total,
        context,
        normed_one,
        inverse_one,
        first_low,
        inner,
        gelu_out,
        normed_two,
        inverse_two,
    ) = saved
    seq_count, rows, width = cotangent.shape
    per_block, blocks = block_sizes(seq_count, rows)
    total = all_kv.shape[1]
    vec_rows = vectors.astype(jnp.float32)
    grad_out = cotangent.reshape(seq_count * rows, width).astype(jnp.float32)
    grad_gain_two = jnp.sum(grad_out * normed_two, 0)
    grad_shift_two = jnp.sum(grad_out, 0)
    grad_h2 = norm_back(grad_out * vec_rows[6], normed_two, inverse_two)
    grad_branch = grad_h2.astype(jnp.bfloat16)
    grad_down_bias = jnp.sum(grad_branch, 0, dtype=jnp.float32)
    grad_w_down = jnp.einsum("nf,nd->fd", gelu_out, grad_branch, preferred_element_type=jnp.float32)
    grad_gelu = jnp.einsum("nd,fd->nf", grad_branch, w_down, preferred_element_type=jnp.float32)
    unused, gelu_pull = jax.vjp(gelu_exact, inner)
    grad_inner = gelu_pull(grad_gelu)[0].astype(jnp.bfloat16)
    grad_b_in = jnp.sum(grad_inner, 0, dtype=jnp.float32)
    grad_w_in = jnp.einsum("nd,nf->df", first_low, grad_inner, preferred_element_type=jnp.float32)
    grad_first = grad_h2 + jnp.einsum(
        "nf,df->nd", grad_inner, w_in, preferred_element_type=jnp.float32
    )
    grad_gain_one = jnp.sum(grad_first * normed_one, 0)
    grad_shift_one = jnp.sum(grad_first, 0)
    grad_h1 = norm_back(grad_first * vec_rows[3], normed_one, inverse_one)
    grad_attn = grad_h1.astype(jnp.bfloat16)
    grad_out_bias = jnp.sum(grad_attn, 0, dtype=jnp.float32)
    grad_w_out = jnp.einsum("nc,nd->cd", context, grad_attn, preferred_element_type=jnp.float32)
    grad_context = jnp.einsum(
        "nd,cd->nc", grad_attn, w_out, preferred_element_type=jnp.float32
    ).astype(jnp.bfloat16)
    grad_query, grad_kv, grad_scores = lax.map(
        attend_back,
        (
            queries.reshape(blocks, per_block, rows, D),
            all_kv.reshape(blocks, per_block, total, 2 * D),
            prev_logits.reshape(blocks, per_block, HEADS, rows, total),
            lengths.reshape(blocks, per_block),
            log_total,
            grad_context.reshape(blocks, per_block, rows, D),
        ),
    )
    kv_summed = lax.psum_scatter(
        grad_kv.reshape(seq_count, total, 2 * D).astype(jnp.bfloat16),
        "seq",
        scatter_dimension=1,
        tiled=True,
    )
    grad_kv_low = kv_summed.reshape(seq_count * rows, 2 * D)
    grad_query = grad_query.reshape(seq_count * rows, D)
    grad_query_bias = jnp.sum(grad_query, 0, dtype=jnp.float32)
    grad_value_bias = jnp.sum(grad_kv_low[:, D:], 0, dtype=jnp.float32)
    grad_qkv = jnp.concatenate([grad_query, grad_kv_low], 1)
    grad_w_qkv = jnp.einsum("nc,nd->cd", tok_rows, grad_qkv, preferred_element_type=jnp.float32)
    grad_tokens = grad_h1 + jnp.einsum(
        "nd,cd->nc", grad_qkv, w_qkv, preferred_element_type=jnp.float32
    )
    grad_vectors = jnp.stack(
        [
            grad_query_bias,
            grad_value_bias,
            grad_out_bias,
            grad_gain_one,
            grad_shift_one,
            grad_down_bias,
            grad_gain_two,
            grad_shift_two,
        ],
        0,
    )
    grad_logits = grad_scores.reshape(seq_count, HEADS, rows, total)
    return (
        grad_tokens,
        grad_logits,
        (grad_w_qkv, grad_w_out, grad_w_in, grad_w_down, grad_b_in, grad_vectors),
    )


def reduce_grads(grads, outer_count):
    grad_w_qkv, grad_w_out, grad_w_in, grad_w_down, grad_b_in, grad_vectors = grads
    terms = (
        grad_w_qkv,
        grad_w_out,
        grad_w_in,
        grad_w_down,
        grad_b_in.reshape(outer_count, -1),
        grad_vectors,
    )
    partial_sum = (
        lax.psum_scatter(terms[0], "dp", scatter_dimension=0, tiled=True),
        lax.psum_scatter(terms[1], "dp", scatter_dimension=0, tiled=True),
        lax.psum_scatter(terms[2], "dp", scatter_dimension=0, tiled=True),
        lax.psum_scatter(terms[3], "dp", scatter_dimension=0, tiled=True),
        lax.psum_scatter(terms[4], "dp", scatter_dimension=0, tiled=True),
        lax.psum_scatter(terms[5], "dp", scatter_dimension=1, tiled=True),
    )
    owned = (
        lax.psum_scatter(
            partial_sum[0].astype(jnp.bfloat16), "seq", scatter_dimension=1, tiled=True
        ).astype(jnp.float32),
        lax.psum_scatter(
            partial_sum[1].astype(jnp.bfloat16), "seq", scatter_dimension=1, tiled=True
        ).astype(jnp.float32),
        lax.psum_scatter(
            partial_sum[2].astype(jnp.bfloat16), "seq", scatter_dimension=1, tiled=True
        ).astype(jnp.float32),
        lax.psum_scatter(
            partial_sum[3].astype(jnp.bfloat16), "seq", scatter_dimension=1, tiled=True
        ).astype(jnp.float32),
        lax.psum_scatter(
            partial_sum[4].astype(jnp.bfloat16), "seq", scatter_dimension=1, tiled=True
        ).astype(jnp.float32),
        lax.psum_scatter(
            partial_sum[5].astype(jnp.bfloat16), "seq", scatter_dimension=0, tiled=True
        ).astype(jnp.float32),
    )
    return (owned[0], owned[1], owned[2], owned[3], owned[4].reshape(-1), owned[5])


def shards(
    hidden_states, prev_logits, lengths, w_qkv, w_out, w_in, w_down, b_in, vectors, cotangent
):
    weights = gather_weights(w_qkv, w_out, w_in, w_down, b_in, vectors)
    result, saved = forward(weights, hidden_states, prev_logits, lengths)
    weights = gather_weights(w_qkv, w_out, w_in, w_down, b_in, vectors)
    unused_out, saved = forward(weights, hidden_states, prev_logits, lengths)
    grad_tokens, grad_logits, grads = backward(weights, saved, prev_logits, lengths, cotangent)
    owned = reduce_grads(grads, lax.axis_size("dp"))
    hidden_out = result.astype(jnp.bfloat16).reshape(hidden_states.shape)
    grad_hidden = grad_tokens.astype(jnp.bfloat16).reshape(hidden_states.shape)
    return (
        hidden_out,
        grad_hidden,
        grad_logits,
        owned[0],
        owned[1],
        owned[2],
        owned[3],
        owned[4],
        owned[5],
    )


def solution(mesh):
    return jax.shard_map(
        shards,
        mesh=mesh,
        in_specs=(
            P("dp", "seq", None),
            P("dp", None, "seq", None),
            P("dp"),
            P("dp", "seq"),
            P("dp", "seq"),
            P("dp", "seq"),
            P("dp", "seq"),
            P(("dp", "seq")),
            P("seq", "dp"),
            P("dp", "seq", None),
        ),
        out_specs=(
            P("dp", "seq", None),
            P("dp", "seq", None),
            P("dp", None, "seq", None),
            P("dp", "seq"),
            P("dp", "seq"),
            P("dp", "seq"),
            P("dp", "seq"),
            P(("dp", "seq")),
            P("seq", "dp"),
        ),
        check_vma=False,
    )
```

profile of v0, /device:TPU:0, one launch (start us, length us, event | category | flops | bytes accessed | tf_op | source)
XLA Modules:
  0.0 1300.2 jit_solution(15309755305140872039)
XLA Ops:
  22.6 26.5 %all-gather.4 = bf16[8,96,8]{1,2,0:T(8,128)(2,1)S(1)} all-gather(bf16[1,96,8]{1,2,0:T(8,128)(2,1)S(1)} %bitcast.295), channel_id=1, replica_groups=mesh['dp'=8,'seq'=4] {'dp'}, dimensions={0}, use_global_device_ids=true | all-gather | bytes 13824 | tf_op jit(solution)/shard_map/all_gather | solution.py:32
  49.8 34.0 %all-gather.12.cloned.1.call-done = bf16[768,2304]{1,0:T(8,128)(2,1)} async-done(((bf16[96,2304]{1,0:T(8,128)(2,1)}), bf16[768,2304]{1,0:T(8,128)(2,1)}) %all-gather.12.cloned.1.call-update) | async-done | bytes 3538960 | tf_op jit(solution)/shard_map/all_gather | solution.py:27
  99.6 10.9 all_gather.59
  110.6 13.4 %all_gather.63 = bf16[384,768]{0,1:T(8,128)(2,1)} all-gather(bf16[384,192]{0,1:T(8,128)(2,1)} %param.22), channel_id=1, replica_groups=mesh['dp'=8,'seq'=4] {'seq'}, dimensions={1}, use_global_device_ids=true | all-gather | bytes 737280 | tf_op jit(solution)/shard_map/all_gather | solution.py:22
  132.1 26.1 %all-gather.5 = bf16[8,1,384]{2,1,0:T(2,128)(2,1)S(1)} all-gather(bf16[1,1,384]{2,1,0:T(2,128)(2,1)S(1)} %reshape.380), channel_id=3, replica_groups=mesh['dp'=8,'seq'=4] {'dp'}, dimensions={0}, use_global_device_ids=true | all-gather | bytes 6912 | tf_op jit(solution)/shard_map/all_gather | solution.py:31
  161.6 17.5 %all-gather.14.cloned.1.call-done = bf16[8,512,1536]{2,1,0:T(8,128)(2,1)} async-done(((bf16[8,128,1536]{2,1,0:T(8,128)(2,1)}), bf16[8,512,1536]{2,1,0:T(8,128)(2,1)}) %all-gather.14.cloned.1.call-update) | async-done | bytes 12582928 | tf_op jit(solution)/shard_map/all_gather | solution.py:137
  179.1 16.7 %copy.67 = bf16[8,512,1536]{1,2,0:T(8,128)(2,1)} copy(bf16[8,512,1536]{2,1,0:T(8,128)(2,1)} %all-gather.14.cloned.1.call-done) | data formatting | bytes 25165824 | tf_op jit(solution)/shard_map/all_gather | solution.py:137
  197.0 34.9 %while.37 = (s32[]{:T(128)}, bf16[2,4,128,768]{3,2,1,0:T(8,128)(2,1)}, f32[2,4,12,128]{3,2,1,0:T(8,128)S(1)}, bf16[2,4,512,1536]{2,3,1,0:T(8,128)(2,1)}, s32[2,4...) while((s32[]{:T(128)}, ...), condition=%wide.region_11.12_spmd, body=%wide.region_8.11_spmd.sunk | while | flops 837152768 | bytes 82014360 | solution.py:139
  233.2 59.3 %while.36 = (s32[]{:T(128)}, bf16[2,4,128,768]{3,2,1,0:T(8,128)(2,1)}, bf16[2,4,512,1536]{2,3,1,0:T(8,128)(2,1)}, s32[2,4]{1,0:T(2,128)S(1)}, bf16[2,4,128,768]{...) while((s32[]{:T(128)}, bf16[2,4,128,768]{3,2,1,0:T(8,128)(2,1)}, ...), condition=%wide.region_3.4_spmd, body=%wide.region_0.3_spmd.sunk | while | flops 830867968 | bytes 69259408 | solution.py:139
  240.0 13.4 %fusion.205 = (f32[4,12,128]{2,1,0:T(8,128)S(1)}, f32[4,12,128,512]{3,2,1,0:T(8,128)}) fusion(bf16[2,4,12,128,512]{4,3,2,1,0:T(8,128)(2,1)} %get-tuple-element.612, s32[]{:T(128)S(6)} %copy.119, pred[4,512]{1,0:T(4,128)(4,1)S(1)} %iota_compare_fusion.6, bf16[4,128,12,64]{1,3,2,0:T(8,128)(2,1)S(1)} %bitcast.266, bf16[4,512,12,64]{1,3,2,0:T(8,128)(2,1)} %bitcast.264), kind=kOutput, calls=%fused_computation.207.clone.1 | convolution fusion | flops 421528064 | bytes 22833156 | tf_op jit(solution)/shard_map/while/body/eval_jaxpr/sub | solution.py:71
  269.7 13.4 %fusion.205 = (f32[4,12,128]{2,1,0:T(8,128)S(1)}, f32[4,12,128,512]{3,2,1,0:T(8,128)}) fusion(bf16[2,4,12,128,512]{4,3,2,1,0:T(8,128)(2,1)} %get-tuple-element.612, s32[]{:T(128)S(6)} %copy.119, pred[4,512]{1,0:T(4,128)(4,1)S(1)} %iota_compare_fusion.6, bf16[4,128,12,64]{1,3,2,0:T(8,128)(2,1)S(1)} %bitcast.266, bf16[4,512,12,64]{1,3,2,0:T(8,128)(2,1)} %bitcast.264), kind=kOutput, calls=%fused_computation.207.clone.1 | convolution fusion | flops 421528064 | bytes 22833156 | tf_op jit(solution)/shard_map/while/body/eval_jaxpr/sub | solution.py:71
  302.9 36.6 %fusion.57.clone.4 = bf16[1024,3072]{1,0:T(8,128)(2,1)} fusion(f32[3072]{0:T(1024)S(1)} %bitcast.292, bf16[768,3072]{1,0:T(8,128)(2,1)} %all-gather.18.cloned.1.call-done, f32[1024,768]{1,0:T(8,128)S(1)} %copy-done.14, f32[768]{0:T(1024)S(1)} %copy-done.28, f32[768]{0:T(1024)S(1)} %copy-done.27, ...), kind=kOutput, calls=%fused_computation.57.clone.clone.clone.clone.clone.clone.1 | convolution fusion | flops 5043388416 | bytes 14182400 | tf_op jit(solution)/shard_map/dot_general | solution.py:154
  339.5 43.8 %all-gather.20.cloned.1.call-done = bf16[3072,768]{0,1:T(8,128)(2,1)} async-done(((bf16[384,768]{0,1:T(8,128)(2,1)}), bf16[3072,768]{0,1:T(8,128)(2,1)}) %all-gather.20.cloned.1.call-update) | async-done | bytes 4718608 | tf_op jit(solution)/shard_map/all_gather | solution.py:30
  383.4 9.6 fusion.122
  393.0 35.2 %multiply_convert_fusion.2 = (bf16[1024,3072]{1,0:T(8,128)(2,1)S(1)}, f32[1024,3072]{1,0:T(8,128)}, f32[1024,3072]{1,0:T(8,128)}) fusion(f32[3072]{0:T(1024)S(1)} %bitcast.293, bf16[768,3072]{1,0:T(8,128)(2,1)S(1)} %copy-done.45, f32[1024,768]{1,0:T(8,128)S(1)} %copy-done.5, f32[1024]{0:T(1024)S(1)} %copy-done.25, f32[1024]{0:T(1024)S(1)} %copy-done.24, ...), kind=kOutput, calls=%fused_computation.61 | convolution fusion | flops 5043388416 | bytes 39348224 | tf_op jit(solution)/shard_map/dot_general | solution.py:154
  440.9 18.5 %convert_reduce_fusion = (f32[3072]{0:T(1024)}, bf16[1024,3072]{1,0:T(8,128)(2,1)}) fusion(f32[1024,3072]{1,0:T(8,128)} %get-tuple-element.368, bf16[3072,768]{0,1:T(8,128)(2,1)} %all-gather.20.cloned.1.call-done, f32[1024,768]{1,0:T(8,128)S(1)} %get-tuple-element.364, f32[1024,3072]{1,0:T(8,128)} %get-tuple-element.388, f32[3072]{0:T(1024)S(1)} %bitcast.294), kind=kOutput, calls=%fused_computation.59 | convolution fusion | flops 4886098944 | bytes 39346176 | tf_op jit(solution)/shard_map/nd,fd->nf/dot_general | solution.py:202
  459.3 10.2 multiply_reduce_fusion.1
  475.8 10.3 fusion.74
  486.2 10.7 fusion.107
  501.6 86.5 %while.38 = (s32[]{:T(128)}, bf16[2,4,128,768]{2,3,1,0:T(8,128)(2,1)}, bf16[2,4,512,1536]{2,3,1,0:T(8,128)(2,1)}, bf16[2,4,12,128,512]{4,3,2,1,0:T(8,128)(2,1)},...) while((s32[]{:T(128)}, ...), condition=%wide.region_22.23_spmd, body=%wide.region_20.22_spmd.sunk | while | flops 2064379904 | bytes 214823344 | solution.py:219
  514.8 9.4 multiply_reduce_fusion.9
  588.1 16.7 %copy.77 = bf16[2,4,512,1536]{3,2,1,0:T(8,128)(2,1)} copy(bf16[2,4,512,1536]{2,3,1,0:T(8,128)(2,1)} %get-tuple-element.137) | data formatting | bytes 25165824 | tf_op jit(solution)/shard_map/convert_element_type | solution.py:231
  606.0 36.8 %all-reduce.1 = bf16[8,384]{1,0:T(8,128)(2,1)S(1)} all-reduce(f32[8,384]{1,0:T(8,128)S(1)} %reshape.357), channel_id=13, replica_groups=mesh['dp'=8,'seq'=4] {'dp'}, use_global_device_ids=true, to_apply=%region_33.34.clone | all-reduce | flops 3072 | bytes 18432
  646.3 63.8 %reduce-scatter.32.cloned.1.call-done = f32[384,768]{1,0:T(8,128)} async-done(((f32[3072,768]{1,0:T(8,128)}), f32[384,768]{1,0:T(8,128)}) %reduce-scatter.32.cloned.1.call-update) | async-done | bytes 1179664 | tf_op jit(solution)/shard_map/reduce_scatter | solution.py:280
  712.5 163.7 %reduce-scatter.28.cloned.1.call-done = f32[96,3072]{1,0:T(8,128)} async-done(((f32[768,3072]{1,0:T(8,128)}), f32[96,3072]{1,0:T(8,128)}) %reduce-scatter.28.cloned.1.call-update) | async-done | bytes 1179664 | tf_op jit(solution)/shard_map/reduce_scatter | solution.py:279
  879.4 97.6 %reduce-scatter.22.cloned.1.call-done = bf16[8,128,1536]{2,1,0:T(8,128)(2,1)} async-done(((bf16[8,512,1536]{2,1,0:T(8,128)(2,1)}), bf16[8,128,1536]{2,1,0:T(8,128)(2,1)}) %reduce-scatter.22.cloned.1.call-update) | async-done | bytes 3145744 | tf_op jit(solution)/shard_map/reduce_scatter | solution.py:230
  1003.6 18.7 %reduce-scatter.36.cloned.1.call-done = bf16[192,96]{1,0:T(8,128)(2,1)} async-done(((bf16[768,96]{1,0:T(8,128)(2,1)}), bf16[192,96]{1,0:T(8,128)(2,1)}) %reduce-scatter.36.cloned.1.call-update) | async-done | bytes 36880
  1023.8 22.9 %reduce-scatter.38.cloned.1.call-done = bf16[192,384]{1,0:T(8,128)(2,1)} async-done(((bf16[768,384]{1,0:T(8,128)(2,1)}), bf16[192,384]{1,0:T(8,128)(2,1)}) %reduce-scatter.38.cloned.1.call-update) | async-done | bytes 147472
  1048.6 22.7 %reduce-scatter.30.cloned.1.call-done = bf16[96,768]{1,0:T(8,128)(2,1)} async-done(((bf16[96,3072]{1,0:T(8,128)(2,1)}), bf16[96,768]{1,0:T(8,128)(2,1)}) %reduce-scatter.30.cloned.1.call-update) | async-done | bytes 147472 | tf_op jit(solution)/shard_map/reduce_scatter | solution.py:291
  1072.9 131.3 %reduce-scatter.34.cloned.1.call-done = f32[96,2304]{1,0:T(8,128)} async-done(((f32[768,2304]{1,0:T(8,128)}), f32[96,2304]{1,0:T(8,128)}) %reduce-scatter.34.cloned.1.call-update) | async-done | bytes 884752
  1215.0 53.2 %reduce-scatter.42.cloned.1.call-done = f32[96,8]{1,0:T(8,128)} async-done(((f32[768,8]{1,0:T(8,128)}), f32[96,8]{1,0:T(8,128)}) %reduce-scatter.42.cloned.1.call-update) | async-done | bytes 3088
  1275.3 16.5 %reduce-scatter.24.cloned.1.call-done = bf16[96,576]{0,1:T(8,128)(2,1)} async-done(((bf16[96,2304]{0,1:T(8,128)(2,1)}), bf16[96,576]{0,1:T(8,128)(2,1)}) %reduce-scatter.24.cloned.1.call-update) | async-done | bytes 110608 | tf_op jit(solution)/shard_map/reduce_scatter | solution.py:285
  (323 shorter events, 283.4 us)
Async XLA Ops:
  7.2 76.6 %all-gather.12.cloned.1.call-start = ((), (), s32[]{:S(2)}) async-start(), calls=%async_computation.11 | async-start | bytes 3981312 | tf_op jit(solution)/shard_map/all_gather | solution.py:27
  17.3 161.7 %all-gather.14.cloned.1.call-start = ((), (), s32[]{:S(2)}) async-start(), calls=%async_computation.12 | async-start | bytes 15728640 | tf_op jit(solution)/shard_map/all_gather | solution.py:137
  49.8 109.0 %copy-start.29 = (f32[768]{0:T(1024)}, f32[768]{0:T(1024)S(1)}, u32[]{:S(2)}) copy-start(f32[768]{0:T(1024)S(1)} %get-tuple-element.307) | copy-start | bytes 9220
  92.8 31.3 %copy-start.49 = (s32[8]{0:T(128)S(1)}, s32[8]{0:T(128)}, u32[]{:S(2)}) copy-start(s32[8]{0:T(128)} %param.18) | copy-start | bytes 100
  92.8 31.3 %copy-start.44 = (u32[32]{0:T(128)S(1)}, u32[32]{0:T(128)}, u32[]{:S(2)}) copy-start(u32[32]{0:T(128)} %constant.157) | copy-start | bytes 388
  92.8 32.6 %copy-start.50 = (bf16[96]{0:T(256)(128)(2,1)S(1)}, bf16[96]{0:T(256)(128)(2,1)}, u32[]{:S(2)}) copy-start(bf16[96]{0:T(256)(128)(2,1)} %param.23) | copy-start | bytes 580
  92.8 66.1 %copy-start.6 = (bf16[8,128,768]{2,1,0:T(8,128)(2,1)S(1)}, bf16[8,128,768]{2,1,0:T(8,128)(2,1)}, u32[]{:S(2)}) copy-start(bf16[8,128,768]{2,1,0:T(8,128)(2,1)} %param.25) | copy-start | bytes 4718596
  92.8 199.6 %all-gather.16.cloned.1.call-start = ((), (), s32[]{:S(2)}) async-start(), calls=%async_computation.13 | async-start | bytes 1327104 | tf_op jit(solution)/shard_map/all_gather | solution.py:28
  99.6 203.3 %all-gather.18.cloned.1.call-start = ((), (), s32[]{:S(2)}) async-start(), calls=%async_computation.14 | async-start | bytes 5308416 | tf_op jit(solution)/shard_map/all_gather | solution.py:29
  110.5 272.8 %all-gather.20.cloned.1.call-start = ((), (), s32[]{:S(2)}) async-start(), calls=%async_computation.15 | async-start | bytes 5308416 | tf_op jit(solution)/shard_map/all_gather | solution.py:30
  124.0 520.4 %reduce-scatter.26.cloned.1.call-start = ((), (), s32[]{:S(2)}) async-start(), calls=%async_computation.18 | async-start | bytes 2654208 | tf_op jit(solution)/shard_map/reduce_scatter | solution.py:278
  233.2 59.3 %copy-start.41 = (f32[768]{0:T(1024)S(1)}, f32[768]{0:T(1024)}, u32[]{:S(2)}) copy-start(f32[768]{0:T(1024)} %get-tuple-element.312) | copy-start | bytes 9220
  302.9 80.4 %copy-start.40 = (f32[768]{0:T(1024)S(1)}, f32[768]{0:T(1024)}, u32[]{:S(2)}) copy-start(f32[768]{0:T(1024)} %get-tuple-element.309) | copy-start | bytes 9220
  383.3 9.6 copy-start.24
  383.3 9.6 copy-start.25
  383.3 9.6 copy-start.45
  383.3 44.8 %slice-start = ((s8[4718592]{0:T(1024)(128)(4,1)}), s8[4194304]{0:T(1024)(128)(4,1)S(1)}, s32[]{:S(2)}) async-start(s8[4718592]{0:T(1024)(128)(4,1)} %bitcast.298), calls=%async_computation.27 | async-start | bytes 8388608
  393.0 35.2 %slice-start.1 = ((s8[4718592]{0:T(1024)(128)(4,1)}), s8[524288]{0:T(1024)(128)(4,1)S(1)}, s32[]{:S(2)}) async-start(s8[4718592]{0:T(1024)(128)(4,1)} %bitcast.298), calls=%async_computation.28 | async-start | bytes 1048576
  440.9 18.5 %copy-start.17 = (f32[1024,768]{1,0:T(8,128)}, f32[1024,768]{1,0:T(8,128)S(1)}, u32[]{:S(2)}) copy-start(f32[1024,768]{1,0:T(8,128)S(1)} %get-tuple-element.364) | copy-start | bytes 9437188
  475.8 234.2 %reduce-scatter.32.cloned.1.call-start = ((), (), s32[]{:S(2)}) async-start(), calls=%async_computation.21 | async-start | bytes 10616832 | tf_op jit(solution)/shard_map/reduce_scatter | solution.py:280
  486.2 390.0 %reduce-scatter.28.cloned.1.call-start = ((), (), s32[]{:S(2)}) async-start(), calls=%async_computation.19 | async-start | bytes 10616832 | tf_op jit(solution)/shard_map/reduce_scatter | solution.py:279
  497.0 480.0 %reduce-scatter.22.cloned.1.call-start = ((), (), s32[]{:S(2)}) async-start(), calls=%async_computation.16 | async-start | bytes 15728640 | tf_op jit(solution)/shard_map/reduce_scatter | solution.py:230
  604.8 273.6 %copy-start.12 = (bf16[2,4,128,768]{2,3,1,0:T(8,128)(2,1)S(1)}, bf16[2,4,128,768]{2,3,1,0:T(8,128)(2,1)}, u32[]{:S(2)}) copy-start(bf16[2,4,128,768]{2,3,1,0:T(8,128)(2,1)} %get-tuple-element.136) | copy-start | bytes 4718596
  604.8 394.6 %reduce-scatter.40.cloned.1.call-start = ((), (), s32[]{:S(2)}) async-start(), calls=%async_computation.25 | async-start | bytes 122880
  644.3 378.0 %reduce-scatter.36.cloned.1.call-start = ((), (), s32[]{:S(2)}) async-start(), calls=%async_computation.23 | async-start | bytes 245760
  646.2 400.5 %reduce-scatter.38.cloned.1.call-start = ((), (), s32[]{:S(2)}) async-start(), calls=%async_computation.24 | async-start | bytes 737280
  712.4 358.9 %reduce-scatter.30.cloned.1.call-start = ((), (), s32[]{:S(2)}) async-start(), calls=%async_computation.20 | async-start | bytes 737280 | tf_op jit(solution)/shard_map/reduce_scatter | solution.py:291
  878.4 325.8 %reduce-scatter.34.cloned.1.call-start = ((), (), s32[]{:S(2)}) async-start(), calls=%async_computation.22 | async-start | bytes 7962624
  879.4 106.8 %copy-start.18 = (bf16[2,4,128,768]{3,2,1,0:T(8,128)(2,1)}, bf16[2,4,128,768]{3,2,1,0:T(8,128)(2,1)S(1)}, u32[]{:S(2)}) copy-start(bf16[2,4,128,768]{3,2,1,0:T(8,128)(2,1)S(1)} %copy.76) | copy-start | bytes 4718596
  994.3 273.9 %reduce-scatter.42.cloned.1.call-start = ((), (), s32[]{:S(2)}) async-start(), calls=%async_computation.26 | async-start | bytes 442368
  996.0 210.5 %copy-start.16 = (f32[1024,768]{1,0:T(8,128)S(1)}, f32[1024,768]{1,0:T(8,128)}, u32[]{:S(2)}) copy-start(f32[1024,768]{1,0:T(8,128)} %copy-done.15) | copy-start | bytes 9437188
  1003.0 288.7 %reduce-scatter.24.cloned.1.call-start = ((), (), s32[]{:S(2)}) async-start(), calls=%async_computation.17 | async-start | bytes 737280 | tf_op jit(solution)/shard_map/reduce_scatter | solution.py:285
  (48 other events, 157.2 us)
Sparse Core Ops, SparseCore 0:
  17.4 66.2 all-gather.11
  92.9 86.0 all-gather.13
  181.8 39.5 all-gather.15
  223.5 78.6 all-gather.17
  304.1 79.1 all-gather.19
  475.9 67.3 reduce-scatter.25
  546.9 163.1 reduce-scatter.31
  713.6 162.5 reduce-scatter.27
  878.8 98.1 reduce-scatter.21
  979.9 19.5 reduce-scatter.39
  1002.5 19.7 reduce-scatter.35
  1024.6 22.0 reduce-scatter.37
  1049.2 22.0 reduce-scatter.29
  1074.8 129.3 reduce-scatter.33
  1207.7 60.4 reduce-scatter.41
  1270.7 21.0 reduce-scatter.23
where the time goes:
time: 1310 us; the launch traced here: 1300 us
  waiting for transfers between devices  689 us (53%)
  matrix products  280 us (21%)
  blocking collectives  145 us (11%)
  local copies, waits for them, and re-layouts  112 us (9%)
  other arithmetic  55.4 us (4%)
  between operations  16.2 us (1%)
    unnamed x21, waiting for transfers between devices  230 us
    reduce_scatter x1, waiting for transfers between devices, reduce_grads(): lax.psum_scatter(terms[2], 'dp', scatter_dimension=0, tiled=True)  164 us
    reduce_scatter x1, waiting for transfers between devices, backward(): lax.psum_scatter(grad_kv.reshape(seq_count, total, 2 * D).astype(jnp.bflo...  97.6 us
    dot_general x2, matrix products, forward(): jnp.dot(first_low, w_in, preferred_element_type=jnp.float32)  71.8 us
    reduce_scatter x1, waiting for transfers between devices, reduce_grads(): lax.psum_scatter(terms[3], 'dp', scatter_dimension=0, tiled=True)  63.8 us
    unnamed x3, blocking collectives  48.9 us
    all_gather x1, waiting for transfers between devices, gather_weights(): lax.all_gather(inner_part[3], 'dp', axis=0, tiled=True)  43.8 us
    all_gather x1, waiting for transfers between devices, gather_weights(): lax.all_gather(inner_part[0], 'dp', axis=0, tiled=True)  34 us
  transfers between devices with their start and end apart: 16, of which 13 were waited for; matrix products, arithmetic and copies ran while one was open for 26% of the time, Pallas kernels for 0%

commit v1 on v0

v1 whole, which is shorter than its diff:
```python
import functools

import jax
import jax.numpy as jnp
from jax import lax
from jax.experimental import pallas as pl
from jax.experimental.pallas import tpu as pltpu
from jax.sharding import PartitionSpec as P

D = 768
HEADS = 12
HEAD_DIM = 64
PAIRS = HEADS // 2
PAIR = 2 * HEAD_DIM
SCALE = HEAD_DIM ** (-0.5)
BF = jnp.bfloat16
F32 = jnp.float32
BOTH = ("dp", "seq")
MIB = 1 << 20


def mm(a, b):
    return lax.dot_general(a, b, (((1,), (0,)), ((), ())), preferred_element_type=F32)


def mm_nt(a, b):
    return lax.dot_general(a, b, (((1,), (1,)), ((), ())), preferred_element_type=F32)


def mm_tn(a, b):
    return lax.dot_general(a, b, (((0,), (0,)), ((), ())), preferred_element_type=F32)


def stack_heads(pair):
    lane = lax.broadcasted_iota(jnp.int32, pair.shape, 1)
    zero = jnp.zeros_like(pair)
    return jnp.concatenate(
        [jnp.where(lane < HEAD_DIM, pair, zero), jnp.where(lane < HEAD_DIM, zero, pair)], 0
    )


def pick_heads(stacked):
    rows = stacked.shape[0] // 2
    lane = lax.broadcasted_iota(jnp.int32, (rows, PAIR), 1)
    return jnp.where(lane < HEAD_DIM, stacked[:rows], stacked[rows:])


def attend_kernel(blocks, order_ref, len_ref, q_ref, *refs):
    kv_refs = refs[:blocks]
    prev_ref, ctx_ref, probs_ref, kv_all = refs[blocks:]
    rows = q_ref.shape[1]
    total = kv_all.shape[0]
    for j in range(blocks):
        start = pl.multiple_of(order_ref[j] * rows, rows)
        kv_all[pl.ds(start, rows), :] = kv_refs[j][0]
    valid = len_ref[pl.program_id(0)]
    key_pos = lax.broadcasted_iota(jnp.int32, (1, total), 1)
    padding = jnp.where(key_pos < valid, 0.0, -1e9)
    for i in range(PAIRS):
        cols = slice(i * PAIR, (i + 1) * PAIR)
        vcols = slice(D + i * PAIR, D + (i + 1) * PAIR)
        query = stack_heads(q_ref[0, :, cols])
        raw = mm_nt(query, kv_all[:, cols])
        prev = prev_ref[0, 2 * i : 2 * i + 2].reshape(2 * rows, total).astype(F32)
        raw = raw + prev + padding
        largest = jnp.max(raw, -1, keepdims=True)
        expo = jnp.exp(raw - largest)
        summed = jnp.sum(expo, -1, keepdims=True)
        probs = (expo * (1.0 / summed)).astype(BF)
        probs_ref[0, 2 * i : 2 * i + 2] = probs.reshape(2, rows, total)
        ctx_ref[0, :, cols] = pick_heads(mm(probs, kv_all[:, vcols])).astype(BF)


def attend(order, lengths, queries, kv_blocks, prev_logits):
    seqs, rows, _ = queries.shape
    blocks = len(kv_blocks)
    total = prev_logits.shape[-1]
    row_spec = lambda width: pl.BlockSpec((1, rows, width), lambda b, *_: (b, 0, 0))
    head_spec = pl.BlockSpec((1, HEADS, rows, total), lambda b, *_: (b, 0, 0, 0))
    return pl.pallas_call(
        functools.partial(attend_kernel, blocks),
        grid_spec=pltpu.PrefetchScalarGridSpec(
            num_scalar_prefetch=2,
            grid=(seqs,),
            in_specs=[row_spec(D)] + [row_spec(2 * D)] * blocks + [head_spec],
            out_specs=[row_spec(D), head_spec],
            scratch_shapes=[pltpu.VMEM((total, 2 * D), BF)],
        ),
        out_shape=[
            jax.ShapeDtypeStruct(queries.shape, BF),
            jax.ShapeDtypeStruct(prev_logits.shape, BF),
        ],
        compiler_params=pltpu.CompilerParams(vmem_limit_bytes=48 * MIB),
        cost_estimate=pl.CostEstimate(
            flops=4 * seqs * HEADS * rows * total * PAIR,
            bytes_accessed=4 * seqs * HEADS * rows * total,
            transcendentals=seqs * HEADS * rows * total,
        ),
    )(order, lengths, queries, *kv_blocks, prev_logits)


def attend_back_kernel(blocks, order_ref, q_ref, *refs):
    kv_refs = refs[:blocks]
    probs_ref, dctx_ref, dlogits_ref, dq_ref = refs[blocks : blocks + 4]
    dkv_refs = refs[blocks + 4 : 2 * blocks + 4]
    kv_all, dkv_all = refs[2 * blocks + 4 :]
    rows = q_ref.shape[1]
    total = kv_all.shape[0]
    starts = [pl.multiple_of(order_ref[j] * rows, rows) for j in range(blocks)]
    for j in range(blocks):
        kv_all[pl.ds(starts[j], rows), :] = kv_refs[j][0]
    for i in range(PAIRS):
        cols = slice(i * PAIR, (i + 1) * PAIR)
        vcols = slice(D + i * PAIR, D + (i + 1) * PAIR)
        query = stack_heads(q_ref[0, :, cols])
        dctx = stack_heads(dctx_ref[0, :, cols])
        probs = probs_ref[0, 2 * i : 2 * i + 2].reshape(2 * rows, total)
        dprobs = mm_nt(dctx, kv_all[:, vcols])
        wide = probs.astype(F32)
        prod = wide * dprobs
        weighted = jnp.sum(prod, -1, keepdims=True)
        dlogits = (prod - wide * weighted).astype(BF)
        dlogits_ref[0, 2 * i : 2 * i + 2] = dlogits.reshape(2, rows, total)
        dq_ref[0, :, cols] = (pick_heads(mm(dlogits, kv_all[:, cols])) * SCALE).astype(BF)
        dkv_all[:, cols] = mm_tn(dlogits, query).astype(BF)
        dkv_all[:, vcols] = mm_tn(probs, dctx).astype(BF)
    for j in range(blocks):
        dkv_refs[j][0] = dkv_all[pl.ds(starts[j], rows), :]


def attend_back(order, queries, kv_blocks, probs, dctx):
    seqs, rows, _ = queries.shape
    blocks = len(kv_blocks)
    total = probs.shape[-1]
    row_spec = lambda width: pl.BlockSpec((1, rows, width), lambda b, *_: (b, 0, 0))
    head_spec = pl.BlockSpec((1, HEADS, rows, total), lambda b, *_: (b, 0, 0, 0))
    outs = pl.pallas_call(
        functools.partial(attend_back_kernel, blocks),
        grid_spec=pltpu.PrefetchScalarGridSpec(
            num_scalar_prefetch=1,
            grid=(seqs,),
            in_specs=[row_spec(D)] + [row_spec(2 * D)] * blocks + [head_spec, row_spec(D)],
            out_specs=[head_spec, row_spec(D)] + [row_spec(2 * D)] * blocks,
            scratch_shapes=[pltpu.VMEM((total, 2 * D), BF), pltpu.VMEM((total, 2 * D), BF)],
        ),
        out_shape=[
            jax.ShapeDtypeStruct(probs.shape, BF),
            jax.ShapeDtypeStruct(queries.shape, BF),
        ]
        + [jax.ShapeDtypeStruct((seqs, rows, 2 * D), BF)] * blocks,
        compiler_params=pltpu.CompilerParams(vmem_limit_bytes=48 * MIB),
        cost_estimate=pl.CostEstimate(
            flops=8 * seqs * HEADS * rows * total * PAIR,
            bytes_accessed=4 * seqs * HEADS * rows * total,
            transcendentals=0,
        ),
    )(order, queries, *kv_blocks, probs, dctx)
    return outs[0], outs[1], outs[2:]


def gelu_and_slope(values):
    size = jnp.abs(values)
    bell = jnp.exp(values * values * -0.5)
    t = 1.0 / (1.0 + (0.3275911 * 0.7071067811865476) * size)
    tail = (0.5 * 1.061405429) * t + (0.5 * -1.453152027)
    tail = tail * t + (0.5 * 1.421413741)
    tail = tail * t + (0.5 * -0.284496736)
    tail = tail * t + (0.5 * 0.254829592)
    tail = tail * t * bell
    cdf = jnp.where(values >= 0.0, 1.0 - tail, tail)
    return values * cdf, cdf + values * bell * 0.3989422804014327


def norm(values):
    average = jnp.mean(values, -1, keepdims=True)
    centred = values - average
    inverse = lax.rsqrt(jnp.mean(centred * centred, -1, keepdims=True) + 1e-06)
    return centred * inverse, inverse


def norm_back(grad, normed, inverse):
    first = jnp.mean(grad, -1, keepdims=True)
    second = jnp.mean(grad * normed, -1, keepdims=True)
    return inverse * (grad - first - normed * second)


def middle_kernel(
    x_ref, ctx_ref, cot_ref, w_out_ref, w_in_ref, w_down_ref, vec_ref, b_in_ref,
    out_ref, dh1_ref, dctx_ref, act_ref, dinner_ref, dbranch_ref, y1_ref, dattn_ref,
    dvec_ref, db_in_ref,
):
    @pl.when(pl.program_id(0) == 0)
    def _():
        dvec_ref[...] = jnp.zeros_like(dvec_ref)
        db_in_ref[...] = jnp.zeros_like(db_in_ref)

    vec = lambda i: vec_ref[i : i + 1, :].astype(F32)
    total = lambda v: jnp.sum(v, 0, keepdims=True)
    h1 = x_ref[...].astype(F32) + (mm(ctx_ref[...], w_out_ref[...]) + vec(2))
    normed1, inverse1 = norm(h1)
    y1 = normed1 * vec(3) + vec(4)
    y1_low = y1.astype(BF)
    y1_ref[...] = y1_low
    inner = mm(y1_low, w_in_ref[...]) + b_in_ref[...].astype(F32)
    act, slope = gelu_and_slope(inner)
    act = act.astype(BF)
    act_ref[...] = act
    h2 = y1 + (mm_nt(act, w_down_ref[...]) + vec(5))
    normed2, inverse2 = norm(h2)
    out_ref[...] = (normed2 * vec(6) + vec(7)).astype(BF)
    cot = cot_ref[...].astype(F32)
    dh2 = norm_back(cot * vec(6), normed2, inverse2)
    dbranch = dh2.astype(BF)
    dbranch_ref[...] = dbranch
    dinner = (mm(dbranch, w_down_ref[...]) * slope).astype(BF)
    dinner_ref[...] = dinner
    dy1 = dh2 + mm_nt(dinner, w_in_ref[...])
    dh1 = norm_back(dy1 * vec(3), normed1, inverse1)
    dh1_ref[...] = dh1
    dattn = dh1.astype(BF)
    dattn_ref[...] = dattn
    dctx_ref[...] = mm_nt(dattn, w_out_ref[...]).astype(BF)
    db_in_ref[...] += total(dinner.astype(F32))
    dvec_ref[2:3, :] += total(dattn.astype(F32))
    dvec_ref[3:4, :] += total(dy1 * normed1)
    dvec_ref[4:5, :] += total(dy1)
    dvec_ref[5:6, :] += total(dbranch.astype(F32))
    dvec_ref[6:7, :] += total(cot * normed2)
    dvec_ref[7:8, :] += total(cot)


def middle(x, ctx, cot, w_out, w_in, w_down_t, vectors, b_in):
    tokens = x.shape[0]
    ff = w_in.shape[1]
    step = 256
    rows = lambda width: pl.BlockSpec((step, width), lambda i: (i, 0))
    whole = lambda a: pl.BlockSpec(a.shape, lambda i: (0, 0), pipeline_mode=pl.Buffered(1))
    sds = jax.ShapeDtypeStruct
    return pl.pallas_call(
        middle_kernel,
        grid=(tokens // step,),
        in_specs=[rows(D)] * 3 + [whole(a) for a in (w_out, w_in, w_down_t, vectors, b_in)],
        out_specs=[rows(D)] * 3
        + [rows(ff)] * 2
        + [rows(D)] * 3
        + [pl.BlockSpec((8, D), lambda i: (0, 0)), pl.BlockSpec((1, ff), lambda i: (0, 0))],
        out_shape=[
            sds((tokens, D), BF),
            sds((tokens, D), F32),
            sds((tokens, D), BF),
            sds((tokens, ff), BF),
            sds((tokens, ff), BF),
            sds((tokens, D), BF),
            sds((tokens, D), BF),
            sds((tokens, D), BF),
            sds((8, D), F32),
            sds((1, ff), F32),
        ],
        compiler_params=pltpu.CompilerParams(vmem_limit_bytes=56 * MIB),
        cost_estimate=pl.CostEstimate(
            flops=tokens * (8 * D * ff + 4 * D * D),
            bytes_accessed=40 * MIB,
            transcendentals=2 * tokens * ff,
        ),
    )(x, ctx, cot, w_out, w_in, w_down_t, vectors, b_in)


def gather_weights(w_qkv, w_out, w_in, w_down, b_in, vectors):
    rows = w_qkv.shape[0]
    small = jnp.concatenate([vectors.reshape(-1), b_in])
    small = jnp.pad(small, (0, D - small.shape[0])).reshape(1, D)
    packed = jnp.concatenate(
        [
            jnp.concatenate([w_qkv, w_out], 1),
            w_in,
            w_down.T.reshape(rows, D),
            small,
        ],
        0,
    )
    dp, seq = lax.axis_size("dp"), lax.axis_size("seq")
    whole = lax.all_gather(packed, BOTH, axis=0, tiled=False).reshape(dp, seq, -1, D)
    both = whole[:, :, :rows]
    wide = w_qkv.shape[1]
    full = lambda a: a.transpose(0, 2, 1, 3).reshape(dp * rows, -1)
    f_qkv = full(both[..., :wide])
    f_out = full(both[..., wide:])
    f_in = full(whole[:, :, rows : 2 * rows])
    down = whole[:, :, 2 * rows : 3 * rows].reshape(dp, seq, w_down.shape[1], w_down.shape[0])
    f_down_t = down.transpose(1, 2, 0, 3).reshape(seq * w_down.shape[1], dp * w_down.shape[0])
    last = whole[:, :, 3 * rows]
    nv = vectors.size
    f_vec = last[..., :nv].reshape((dp, seq) + vectors.shape)
    f_vec = f_vec.transpose(1, 2, 0, 3).reshape(seq * vectors.shape[0], dp * vectors.shape[1])
    f_b = last[..., nv : nv + b_in.shape[0]].reshape(1, -1)
    return f_qkv, f_out, f_in, f_down_t, f_b, f_vec


def reduce_grads(g_qkv, g_out, g_in, g_down_t, g_b, g_vec):
    dp, seq = lax.axis_size("dp"), lax.axis_size("seq")
    rows = D // dp
    split = lambda a: a.reshape(dp, a.shape[0] // dp, seq, -1).transpose(0, 2, 1, 3)
    both = jnp.concatenate([split(g_qkv), split(g_out)], 3)
    ff = g_in.shape[1]
    down = g_down_t.reshape(seq, D // seq, dp, ff // dp).transpose(2, 0, 1, 3)
    vec = g_vec.reshape(seq, 8 // seq, dp, rows).transpose(2, 0, 1, 3).reshape(dp, seq, -1)
    small = jnp.concatenate([vec, g_b.reshape(dp, seq, -1)], 2)
    width = small.shape[2]
    small = jnp.pad(small, ((0, 0), (0, 0), (0, D - width))).reshape(dp, seq, 1, D)
    packed = jnp.concatenate(
        [both, split(g_in), down.reshape(dp, seq, rows, D), small.astype(BF)], 2
    )
    mine = lax.psum_scatter(
        packed.reshape(dp * seq, -1, D), BOTH, scatter_dimension=0, tiled=True
    )[0].astype(F32)
    wide = 3 * D // seq
    o_down = mine[2 * rows : 3 * rows].reshape(D // seq, ff // dp).T
    last = mine[3 * rows]
    nv = 8 * D // (dp * seq)
    return (
        mine[:rows, :wide],
        mine[:rows, wide:],
        mine[rows : 2 * rows],
        o_down,
        last[nv : nv + ff // (dp * seq)],
        last[:nv].reshape(8 // seq, rows),
    )


def shards(
    hidden_states, prev_logits, lengths, w_qkv, w_out, w_in, w_down, b_in, vectors, cotangent
):
    seqs, rows, _ = hidden_states.shape
    tokens = seqs * rows
    seq = lax.axis_size("seq")
    me = lax.axis_index("seq")
    f_qkv, f_out, f_in, f_down_t, f_b, f_vec = gather_weights(
        w_qkv, w_out, w_in, w_down, b_in, vectors
    )
    order = jnp.arange(seq, dtype=jnp.int32) ^ me
    x_blocks = [hidden_states]
    for j in range(1, seq):
        x_blocks.append(lax.ppermute(hidden_states, "seq", [(a, a ^ j) for a in range(seq)]))
    x_rows = [b.reshape(tokens, D) for b in x_blocks]
    vec = f_vec.astype(F32)
    f_kv = f_qkv[:, D:]
    queries = ((mm(x_rows[0], f_qkv[:, :D]) + vec[0]).astype(BF) * SCALE).astype(BF)
    queries = queries.reshape(seqs, rows, D)
    kv_bias = jnp.concatenate([jnp.zeros((D,), F32), vec[1]])
    kv_blocks = [(mm(b, f_kv) + kv_bias).astype(BF).reshape(seqs, rows, 2 * D) for b in x_rows]
    ctx, probs = attend(order, lengths, queries, kv_blocks, prev_logits)
    out, dh1, dctx, act, dinner, dbranch, y1, dattn, dvec, db_in = middle(
        x_rows[0],
        ctx.reshape(tokens, D),
        cotangent.reshape(tokens, D),
        f_out,
        f_in,
        f_down_t,
        f_vec,
        f_b,
    )
    g_down_t = mm_tn(dbranch, act).astype(BF)
    g_in = mm_tn(y1, dinner).astype(BF)
    g_out = mm_tn(ctx.reshape(tokens, D), dattn).astype(BF)
    dlogits, dq, dkv = attend_back(
        order, queries, kv_blocks, probs, dctx.reshape(seqs, rows, D)
    )
    dq = dq.reshape(tokens, D)
    dkv = [b.reshape(tokens, 2 * D) for b in dkv]
    g_q = mm_tn(x_rows[0], dq)
    g_kv = sum(mm_tn(a, b) for a, b in zip(x_rows, dkv))
    g_qkv = jnp.concatenate([g_q, g_kv], 1).astype(BF)
    dx = [mm_nt(b, f_kv) for b in dkv]
    dx_own = dh1 + mm_nt(dq, f_qkv[:, :D]) + dx[0]
    for j in range(1, seq):
        dx_own = dx_own + lax.ppermute(
            dx[j].astype(BF), "seq", [(a, a ^ j) for a in range(seq)]
        ).astype(F32)
    dvec = dvec.at[0].set(jnp.sum(dq, 0, dtype=F32))
    dvec = dvec.at[1].set(sum(jnp.sum(b[:, D:], 0, dtype=F32) for b in dkv))
    owned = reduce_grads(g_qkv, g_out, g_in, g_down_t, db_in, dvec)
    shape = hidden_states.shape
    return (out.reshape(shape), dx_own.astype(BF).reshape(shape), dlogits) + owned


def solution(mesh):
    return jax.shard_map(
        shards,
        mesh=mesh,
        in_specs=(
            P("dp", "seq", None),
            P("dp", None, "seq", None),
            P("dp"),
            P("dp", "seq"),
            P("dp", "seq"),
            P("dp", "seq"),
            P("dp", "seq"),
            P(("dp", "seq")),
            P("seq", "dp"),
            P("dp", "seq", None),
        ),
        out_specs=(
            P("dp", "seq", None),
            P("dp", "seq", None),
            P("dp", None, "seq", None),
            P("dp", "seq"),
            P("dp", "seq"),
            P("dp", "seq"),
            P("dp", "seq"),
            P(("dp", "seq")),
            P("seq", "dp"),
        ),
        check_vma=False,
    )
```

time: 1310 us -> 633 us (0.48)
  waiting for transfers between devices: 689 us -> 284 us
  matrix products: 280 us -> 82.9 us
  blocking collectives: 145 us -> 0 us
  Pallas kernels: 0 us -> 102 us
  other arithmetic: 55.4 us -> 24.8 us
    reduce_scatter x6 -> x1, waiting for transfers between devices: 364 us -> 74.6 us  [reduce_grads(): lax.psum_scatter(packed.reshape(dp * seq, -1, D), BOTH, scatter_dimension...]
    unnamed x21 -> x2, waiting for transfers between devices: 230 us -> 0.03 us
    dot_general x31 -> x18, matrix products: 253 us -> 82.9 us  [the longest x8 41.6 us: mm_tn(): lax.dot_general(a, b, (((0,), (0,)), ((), ())), preferred_element_type=F32)]
    pallas_call x0 -> x3, Pallas kernels: none -> 102 us  [the longest x1 44 us: middle(): pl.pallas_call(middle_kernel, grid=(tokens // step,), in_specs=[rows(D)]...]
    all_gather x7 -> x0, blocking collectives: 96.5 us -> none  [the longest x1 26.5 us: gather_weights(): lax.all_gather(inner_part[5], 'dp', axis=1, tiled=True)]
    ppermute x0 -> x6, waiting for transfers between devices: none -> 78.9 us  [the longest x3 78.9 us: shards(): lax.ppermute(dx[j].astype(BF), 'seq', [(a, a ^ j) for a in range(seq)])]
    unnamed x3 -> x0, blocking collectives: 48.9 us -> none
    reshape x2 -> x19, local copies, waits for them, and re-layouts: 0.09 us -> 36.2 us  [the longest x2 13.2 us: reduce_grads(): a.reshape(dp, a.shape[0] // dp, seq, -1).transpose(0, 2, 1, 3)]
  transfers between devices with their start and end apart: 16 -> 8, of which waited for: 13 -> 4; matrix products, arithmetic and copies ran while one was open for 26% -> 13% of each run, Pallas kernels for 0% -> 0%
where the time goes in v1:
time: 633 us; the launch traced here: 629 us
  waiting for transfers between devices  284 us (45%)
  local copies, waits for them, and re-layouts  115 us (18%)
  Pallas kernels  102 us (16%)
  matrix products  82.9 us (13%)
  other arithmetic  24.8 us (4%)
  between operations  14.8 us (2%)
    all_gather x1, waiting for transfers between devices, gather_weights(): lax.all_gather(packed, BOTH, axis=0, tiled=False).reshape(dp, seq, -1, D)  131 us
    ppermute x3, waiting for transfers between devices, shards(): lax.ppermute(dx[j].astype(BF), 'seq', [(a, a ^ j) for a in range(seq)])  78.9 us
    reduce_scatter x1, waiting for transfers between devices, reduce_grads(): lax.psum_scatter(packed.reshape(dp * seq, -1, D), BOTH, scatter_dimension...  74.6 us
    pallas_call x1, Pallas kernels, middle(): pl.pallas_call(middle_kernel, grid=(tokens // step,), in_specs=[rows(D)]...  44 us
    dot_general x8, matrix products, mm_tn(): lax.dot_general(a, b, (((0,), (0,)), ((), ())), preferred_element_type=F32)  41.6 us
    pallas_call x1, Pallas kernels, attend_back(): pl.pallas_call(functools.partial(attend_back_kernel, blocks), grid_spec=p...  31.4 us
    pallas_call x1, Pallas kernels, attend(): pl.pallas_call(functools.partial(attend_kernel, blocks), grid_spec=pltpu....  26.3 us
    dot_general x5, matrix products, mm(): lax.dot_general(a, b, (((1,), (0,)), ((), ())), preferred_element_type=F32)  25 us
  transfers between devices with their start and end apart: 8, of which 4 were waited for; matrix products, arithmetic and copies ran while one was open for 13% of the time, Pallas kernels for 0%

profile of v1, /device:TPU:0, one launch (start us, length us, event | category | flops | bytes accessed | tf_op | source)
XLA Modules:
  0.0 628.7 jit_solution(2272386217363363042)
XLA Ops:
  14.7 130.8 %all-gather.4.cloned.1.call-done = bf16[32,289,768]{2,1,0:T(8,128)(2,1)} async-done(((bf16[1,289,768]{2,1,0:T(8,128)(2,1)}), bf16[32,289,768]{2,1,0:T(8,128)(2,1)}) %all-gather.4.cloned.1.call-update) | async-done | bytes 14204944 | tf_op jit(solution)/shard_map/all_gather | solution.py:282
  148.8 8.3 %fusion.17 = (bf16[8,4,96,768]{3,2,1,0:T(8,128)(2,1)}, bf16[8,96,4,768]{3,1,2,0:T(8,128)(2,1)}) fusion(bf16[8,4,289,768]{3,2,1,0:T(8,128)(2,1)} %bitcast.158), kind=kLoop, calls=%fused_computation.61 | loop fusion | bytes 18874368 | tf_op jit(solution)/shard_map/slice | solution.py:289
  161.9 8.0 %reshape.250 = bf16[8,4,192,384]{3,2,1,0:T(8,128)(2,1)} reshape(bf16[8,4,96,768]{3,2,1,0:T(8,128)(2,1)} %get-tuple-element.71) | data formatting | bytes 9437184 | tf_op jit(solution)/shard_map/reshape | solution.py:289
  170.0 5.2 copy.99
  181.1 3.9 copy.93
  185.0 7.9 %reshape.235 = bf16[768,2304]{1,0:T(8,128)(2,1)} reshape(bf16[8,96,4,576]{3,2,1,0:T(4,128)(2,1)} %copy.93) | data formatting | bytes 7077888 | tf_op jit(solution)/shard_map/reshape | solution.py:285
  193.0 5.8 add_convert_fusion.3
  201.3 6.5 %add_convert_fusion.1 = bf16[1536,1024]{0,1:T(8,128)(2,1)} fusion(bf16[1024,768]{1,0:T(8,128)(2,1)} %bitcast.14, f32[1536]{0:T(1024)S(1)} %concatenate.42, bf16[768,2304]{1,0:T(8,128)(2,1)} %reshape.235), kind=kOutput, calls=%fused_computation.2 | convolution fusion | flops 2419064832 | bytes 7084032 | tf_op jit(solution)/shard_map/dot_general | solution.py:23
  207.8 5.6 add_convert_fusion.2
  213.4 5.5 add_convert_fusion
  218.9 3.6 copy.98
  225.8 26.3 %shard_map.169 = (bf16[8,128,768]{2,1,0:T(8,128)(2,1)S(1)}, bf16[8,12,128,512]{3,2,1,0:T(8,128)(2,1)}) custom-call(s32[4]{0:T(128)S(1)} %iota_xor_fusion.order_ref, s32[8]{0:T(128)S(1)} %copy-done.1, bf16[8,128,768]{2,1,0:T(8,128)(2,1)S(1)} %bitcast.140, bf16[8,128,1536]{2,1,0:T(8,128)(2,1)} %bitcast.160, bf16[8,128,1536]{2,1,0:T(8,128)(2,1)} %bitcast.164, ...), custom_call_target="tpu_custom_call" | custom-call | flops 3221225472 | bytes 25165824 | tf_op jit(solution)/shard_map/pallas_call | solution.py:80
  253.2 44.0 %shard_map.170 = (bf16[1024,768]{1,0:T(8,128)(2,1)}, f32[1024,768]{1,0:T(8,128)}, bf16[1024,768]{1,0:T(8,128)(2,1)}, bf16[1024,3072]{1,0:T(8,128)(2,1)}, bf16[10...) custom-call(bf16[1024,768]{1,0:T(8,128)(2,1)} %bitcast.188, ...), custom_call_target="tpu_custom_call" | custom-call | flops 21743271936 | bytes 41943040 | tf_op jit(solution)/shard_map/pallas_call | solution.py:239
  298.6 31.4 %shard_map.171 = (bf16[8,12,128,512]{3,2,1,0:T(8,128)(2,1)}, bf16[8,128,768]{2,1,0:T(8,128)(2,1)S(1)}, bf16[8,128,1536]{2,1,0:T(8,128)(2,1)}, bf16[8,128,1536]{2...) custom-call(s32[4]{0:T(128)S(1)} %iota_xor_fusion.order_ref, ...), custom_call_target="tpu_custom_call" | custom-call | flops 6442450944 | bytes 25165824 | tf_op jit(solution)/shard_map/pallas_call | solution.py:137
  335.3 4.3 fusion.19
  342.5 3.5 reshape.261
  346.1 5.3 fusion.20
  351.3 4.3 fusion.21
  355.7 5.0 fusion.1
  362.8 5.8 copy.106
  368.6 9.5 %convert_element_type.111 = bf16[8,96,4,576]{3,2,1,0:T(4,128)(2,1)} reshape(bf16[768,2304]{1,0:T(8,128)(2,1)} %copy.106) | data formatting | bytes 7077888 | tf_op jit(solution)/shard_map/convert_element_type | solution.py:372
  378.1 5.2 pad_maximum_fusion.1
  386.3 9.5 %convolution_convert_fusion.1 = bf16[768,3072]{1,0:T(8,128)(2,1)} fusion(bf16[1024,768]{1,0:T(8,128)(2,1)S(1)} %copy-done.27, bf16[1024,3072]{1,0:T(8,128)(2,1)} %get-tuple-element.64), kind=kOutput, calls=%fused_computation.6 | convolution fusion | flops 4834197504 | bytes 12582912 | tf_op jit(solution)/shard_map/dot_general | solution.py:31
  395.8 9.8 %reshape.262 = bf16[8,96,4,768]{3,2,1,0:T(4,128)(2,1)} reshape(bf16[768,3072]{1,0:T(8,128)(2,1)} %convolution_convert_fusion.1) | data formatting | bytes 9437184 | tf_op jit(solution)/shard_map/reshape | solution.py:302
  405.6 5.6 copy.108
  411.2 8.3 %convolution_convert_fusion = bf16[768,3072]{1,0:T(8,128)(2,1)S(1)} fusion(bf16[1024,768]{1,0:T(8,128)(2,1)S(1)} %copy-done.26, bf16[1024,3072]{1,0:T(8,128)(2,1)} %get-tuple-element.66), kind=kOutput, calls=%fused_computation.5 | convolution fusion | flops 4834197504 | bytes 12582912 | tf_op jit(solution)/shard_map/dot_general | solution.py:31
  424.2 8.0 %concatenate.47 = bf16[32,96,768]{2,1,0:T(8,128)(2,1)} reshape(bf16[8,4,192,384]{3,2,1,0:T(8,128)(2,1)} %copy.109) | data formatting | bytes 9437184 | tf_op jit(solution)/shard_map/concatenate | solution.py:310
  432.2 12.2 %pad_maximum_fusion = bf16[32,289,768]{2,1,0:T(8,128)(2,1)} fusion(bf16[32,1,768]{2,1,0:T(2,128)(2,1)S(1)} %concatenate.51, bf16[32,96,768]{2,1,0:T(8,128)(2,1)} %concatenate.47, bf16[32,96,768]{2,1,0:T(8,128)(2,1)} %bitcast.154, bf16[32,96,768]{2,1,0:T(8,128)(2,1)} %bitcast.153), kind=kLoop, calls=%fused_computation | loop fusion | flops 56819712 | bytes 28409856 | tf_op jit(solution)/shard_map/concatenate | solution.py:310
  444.5 5.4 convolution_convert_fusion.4
  459.8 31.8 %collective-permute-done.5 = bf16[1024,768]{1,0:T(8,128)(2,1)S(1)} collective-permute-done((bf16[1024,768]{1,0:T(8,128)(2,1)S(1)}, bf16[1024,768]{1,0:T(8,128)(2,1)S(1)}, u32[]{:S(2)}, u32[]{:S(2)}) %collective-permute-start.5) | collective-permute-done | bytes 1572896 | tf_op jit(solution)/shard_map/ppermute | solution.py:376
  491.6 47.1 %collective-permute-done.4 = bf16[1024,768]{1,0:T(8,128)(2,1)S(1)} collective-permute-done((bf16[1024,768]{1,0:T(8,128)(2,1)S(1)}, bf16[1024,768]{1,0:T(8,128)(2,1)S(1)}, u32[]{:S(2)}, u32[]{:S(2)}) %collective-permute-start.4) | collective-permute-done | bytes 1572896 | tf_op jit(solution)/shard_map/ppermute | solution.py:376
  541.7 74.6 %reduce-scatter.2.cloned.1.call-done = bf16[1,289,768]{2,1,0:T(8,128)(2,1)} async-done(((bf16[32,289,768]{2,1,0:T(8,128)(2,1)}), bf16[1,289,768]{2,1,0:T(8,128)(2,1)}) %reduce-scatter.2.cloned.1.call-update) | async-done | bytes 443920 | tf_op jit(solution)/shard_map/reduce_scatter | solution.py:313
  (147 shorter events, 66.1 us)
Async XLA Ops:
  7.2 138.3 %all-gather.4.cloned.1.call-start = ((), (), s32[]{:S(2)}) async-start(), calls=%async_computation.2 | async-start | bytes 15003648 | tf_op jit(solution)/shard_map/all_gather | solution.py:282
  11.5 604.7 %reduce-scatter.2.cloned.1.call-start = ((), (), s32[]{:S(2)}) async-start(), calls=%async_computation.1 | async-start | bytes 15003648 | tf_op jit(solution)/shard_map/reduce_scatter | solution.py:313
  11.6 201.8 %collective-permute-start.2 = (bf16[8,128,768]{2,1,0:T(8,128)(2,1)}, bf16[8,128,768]{2,1,0:T(8,128)(2,1)}, u32[]{:S(2)}, u32[]{:S(2)}) collective-permute-start(bf16[8,128,768]{2,1,0:T(8,128)(2,1)} %param.14), channel_id=1, source_target_pairs={{0,3},{1,2},{2,1},{3,0},{4,7},{5,6},{6,5},{7,4},{8,11},{9,10},{10,... | collective-permute-start | bytes 4718600 | tf_op jit(solution)/shard_map/ppermute | solution.py:343
  14.0 187.2 %collective-permute-start.1 = (bf16[8,128,768]{2,1,0:T(8,128)(2,1)}, bf16[8,128,768]{2,1,0:T(8,128)(2,1)}, u32[]{:S(2)}, u32[]{:S(2)}) collective-permute-start(bf16[8,128,768]{2,1,0:T(8,128)(2,1)} %param.14), channel_id=1, source_target_pairs={{0,2},{1,3},{2,0},{3,1},{4,6},{5,7},{6,4},{7,5},{8,10},{9,11},{10,... | collective-permute-start | bytes 4718600 | tf_op jit(solution)/shard_map/ppermute | solution.py:343
  14.7 193.1 %collective-permute-start = (bf16[8,128,768]{2,1,0:T(8,128)(2,1)}, bf16[8,128,768]{2,1,0:T(8,128)(2,1)}, u32[]{:S(2)}, u32[]{:S(2)}) collective-permute-start(bf16[8,128,768]{2,1,0:T(8,128)(2,1)} %param.14), channel_id=1, source_target_pairs={{0,1},{1,0},{2,3},{3,2},{4,5},{5,4},{6,7},{7,6},{8,9},{9,8},{10,11... | collective-permute-start | bytes 4718600 | tf_op jit(solution)/shard_map/ppermute | solution.py:343
  157.3 12.7 %copy-start.19 = (bf16[8,768]{1,0:T(8,128)(2,1)}, bf16[8,768]{1,0:T(8,128)(2,1)S(1)}, u32[]{:S(2)}) copy-start(bf16[8,768]{1,0:T(8,128)(2,1)S(1)} %reshape.237.vec_ref) | copy-start | bytes 36868
  185.0 8.0 %copy-start.22 = (bf16[8,128,768]{2,1,0:T(8,128)(2,1)S(1)}, bf16[8,128,768]{2,1,0:T(8,128)(2,1)}, u32[]{:S(2)}) copy-start(bf16[8,128,768]{2,1,0:T(8,128)(2,1)} %param.14) | copy-start | bytes 4718596
  193.0 5.8 copy-start.4
  193.0 5.8 copy-start.23
  201.3 6.5 %copy-start.5 = (bf16[768,2304]{1,0:T(8,128)(2,1)S(1)}, bf16[768,2304]{1,0:T(8,128)(2,1)}, u32[]{:S(2)}) copy-start(bf16[768,2304]{1,0:T(8,128)(2,1)} %reshape.235) | copy-start | bytes 10616836
  207.8 11.1 %slice-start = ((s8[4718592]{0:T(1024)(128)(4,1)}), s8[4194304]{0:T(1024)(128)(4,1)S(1)}, s32[]{:S(2)}) async-start(s8[4718592]{0:T(1024)(128)(4,1)} %bitcast.151), calls=%async_computation.3 | async-start | bytes 8388608
  213.4 5.5 slice-start.1
  222.6 3.3 copy-start.1
  298.6 31.7 %copy-start.24 = (bf16[8,128,768]{2,1,0:T(8,128)(2,1)S(1)}, bf16[8,128,768]{2,1,0:T(8,128)(2,1)}, u32[]{:S(2)}) copy-start(bf16[8,128,768]{2,1,0:T(8,128)(2,1)} %param.14) | copy-start | bytes 4718596
  335.3 4.6 copy-start.18
  335.3 4.9 copy-start.15
  346.0 5.3 copy-start.16
  346.0 9.6 %slice-start.2 = ((s8[4718592]{0:T(1024)(128)(4,1)}), s8[4194304]{0:T(1024)(128)(4,1)S(1)}, s32[]{:S(2)}) async-start(s8[4718592]{0:T(1024)(128)(4,1)} %bitcast.192), calls=%async_computation.5 | async-start | bytes 8388608
  351.3 4.4 copy-start.13
  351.3 4.4 slice-start.3
  355.7 5.0 copy-start.9
  383.3 3.1 copy-start.27
  405.6 5.6 copy-start.26
  444.5 5.4 copy-start.6
  444.5 5.4 copy-start.17
  449.9 2.7 copy-start.14
  452.6 4.6 copy-start.11
  455.2 83.5 %copy-start.7 = (f32[1024,768]{1,0:T(8,128)S(1)}, f32[1024,768]{1,0:T(8,128)}, u32[]{:S(2)}) copy-start(f32[1024,768]{1,0:T(8,128)} %get-tuple-element.53) | copy-start | bytes 9437188
  455.2 36.4 %collective-permute-start.5 = (bf16[1024,768]{1,0:T(8,128)(2,1)S(1)}, bf16[1024,768]{1,0:T(8,128)(2,1)S(1)}, u32[]{:S(2)}, u32[]{:S(2)}) collective-permute-start(bf16[1024,768]{1,0:T(8,128)(2,1)S(1)} %convolution_convert_fusion.2), channel_id=1, source_target_pairs={{0,3},{1,2},{2,1},{3,0},{4,7},{5,6},{6,5},{7,4},{8,11},{9,10},{10,... | collective-permute-start | bytes 4718600 | tf_op jit(solution)/shard_map/ppermute | solution.py:376
  456.6 82.0 %collective-permute-start.4 = (bf16[1024,768]{1,0:T(8,128)(2,1)S(1)}, bf16[1024,768]{1,0:T(8,128)(2,1)S(1)}, u32[]{:S(2)}, u32[]{:S(2)}) collective-permute-start(bf16[1024,768]{1,0:T(8,128)(2,1)S(1)} %convolution_convert_fusion.3), channel_id=1, source_target_pairs={{0,2},{1,3},{2,0},{3,1},{4,6},{5,7},{6,4},{7,5},{8,10},{9,11},{10,... | collective-permute-start | bytes 4718600 | tf_op jit(solution)/shard_map/ppermute | solution.py:376
  457.2 81.5 %collective-permute-start.3 = (bf16[1024,768]{1,0:T(8,128)(2,1)S(1)}, bf16[1024,768]{1,0:T(8,128)(2,1)S(1)}, u32[]{:S(2)}, u32[]{:S(2)}) collective-permute-start(bf16[1024,768]{1,0:T(8,128)(2,1)S(1)} %convolution_convert_fusion.4), channel_id=1, source_target_pairs={{0,1},{1,0},{2,3},{3,2},{4,5},{5,4},{6,7},{7,6},{8,9},{9,8},{10,11... | collective-permute-start | bytes 4718600 | tf_op jit(solution)/shard_map/ppermute | solution.py:376
  616.3 3.3 copy-start.8
  (8 other events, 16.7 us)
Sparse Core Ops, SparseCore 0:
  11.7 133.8 all-gather.3
  444.6 171.6 reduce-scatter.1

commit v2 on v1

v2 whole, which is shorter than its diff:
```python
import functools

import jax
import jax.numpy as jnp
from jax import lax
from jax.experimental import pallas as pl
from jax.experimental.pallas import tpu as pltpu
from jax.sharding import PartitionSpec as P

D = 768
HEADS = 12
HEAD_DIM = 64
PAIRS = HEADS // 2
PAIR = 2 * HEAD_DIM
SCALE = HEAD_DIM ** (-0.5)
BF = jnp.bfloat16
F32 = jnp.float32
BOTH = ("dp", "seq")
MIB = 1 << 20


def mm(a, b):
    return lax.dot_general(a, b, (((1,), (0,)), ((), ())), preferred_element_type=F32)


def mm_nt(a, b):
    return lax.dot_general(a, b, (((1,), (1,)), ((), ())), preferred_element_type=F32)


def mm_tn(a, b):
    return lax.dot_general(a, b, (((0,), (0,)), ((), ())), preferred_element_type=F32)


def stack_heads(pair):
    lane = lax.broadcasted_iota(jnp.int32, pair.shape, 1)
    zero = jnp.zeros_like(pair)
    return jnp.concatenate(
        [jnp.where(lane < HEAD_DIM, pair, zero), jnp.where(lane < HEAD_DIM, zero, pair)], 0
    )


def pick_heads(stacked):
    rows = stacked.shape[0] // 2
    lane = lax.broadcasted_iota(jnp.int32, (rows, PAIR), 1)
    return jnp.where(lane < HEAD_DIM, stacked[:rows], stacked[rows:])


def swap(a, axis, bit):
    size = lax.axis_size(axis)
    return lax.ppermute(a, axis, [(i, i ^ bit) for i in range(size)])


def swap_core(a):
    return swap(a, "seq", 1)


def swap_x(a):
    return swap(a, "seq", 2)


def swap_y(a):
    return swap(a, "dp", 1)


def shift_z(a, places):
    size = lax.axis_size("dp")
    return lax.ppermute(a, "dp", [(i, (i + 2 * places) % size) for i in range(size)])


def by_pieces():
    return lax.axis_size("dp") == 8 and lax.axis_size("seq") == 4


def place():
    dp, seq = lax.axis_index("dp"), lax.axis_index("seq")
    return dp >> 1, dp & 1, seq >> 1, seq & 1


def gather_pieces(a):
    own = jnp.stack([a] + [shift_z(a, k) for k in range(1, 4)])
    own_x = swap_x(own)
    half = [own, own_x, swap_y(own), swap_y(own_x)]
    return half + [swap_core(b) for b in half]


def piece_table():
    z, y, x, core = place()
    table = []
    for far in range(8):
        for k in range(4):
            table.append(2 * ((z - k) & 3) + (y ^ (far >> 1 & 1)))
            table.append(2 * (x ^ (far & 1)) + (core ^ (far >> 2)))
    return jnp.stack(table).astype(jnp.int32)


def pieces_of(refs, table_ref):
    for a, ref in enumerate(refs):
        depth = ref.shape[0]
        for k in range(depth):
            n = a * depth + k
            yield ref.at[k], table_ref[2 * n], table_ref[2 * n + 1]


def wait_whole(ref, sem):
    pltpu.make_async_copy(ref, ref, sem).wait()


def add(*parts):
    return sum(p.astype(F32) for p in parts)


def low(a):
    return a.astype(BF)


def reduce_pieces(send, keep, first, second):
    got = swap_core(send)
    got_first = first(low(add(keep[1], got[1])))
    got_second = second(low(add(keep[0, 1], got[0, 1], got_first[1])))
    parts = lambda k: add(keep[0, 0, k], got[0, 0, k], got_first[0, k], got_second[k])
    return parts(0) + add(*[shift_z(low(parts(k)), k) for k in range(1, 4)])


def project_kernel(count, table_ref, x0_ref, x1_ref, x2_ref, x3_ref, bias_ref, *refs):
    piece_refs = refs[:count]
    q_ref, kv_ref, w_ref, w_all, stage, sems = refs[count:]
    which, part = pl.program_id(0), pl.program_id(1)
    last = (which == pl.num_programs(0) - 1) & (part == pl.num_programs(1) - 1)
    keep = pltpu.make_async_copy(w_all, w_ref, sems.at[1])

    @pl.when((which == 0) & (part == 0))
    def _():
        if count == 1:
            pltpu.make_async_copy(piece_refs[0], w_all, sems.at[0]).start()
            wait_whole(w_all, sems.at[0])
        else:
            high, wide = stage.shape[1] // 8, stage.shape[2]
            for piece, dp, seq in pieces_of(piece_refs, table_ref):
                rows = pl.ds(pl.multiple_of(dp * high, high), high)
                pltpu.make_async_copy(piece, stage.at[seq, rows], sems.at[0]).start()
            wait_whole(stage, sems.at[0])
            for s in range(4):
                w_all[:, s * wide : (s + 1) * wide] = stage[s]
        keep.start()

    for j, x_ref in enumerate((x0_ref, x1_ref, x2_ref, x3_ref)):

        @pl.when(which == j)
        def _():
            rows = x_ref[...]
            kv_ref[0, :, :D] = mm(rows, w_all[:, D : 2 * D]).astype(BF)
            kv_ref[0, :, D:] = (mm(rows, w_all[:, 2 * D :]) + bias_ref[1:2]).astype(BF)
            if j == 0:
                query = (mm(rows, w_all[:, :D]) + bias_ref[0:1]).astype(BF)
                q_ref[...] = query * SCALE

    @pl.when(last)
    def _():
        keep.wait()


def project(table, x_blocks, bias, pieces):
    tokens = x_blocks[0].shape[0]
    step = 512
    parts = tokens // step

    def x_spec(j):
        return pl.BlockSpec(
            (step, D),
            lambda i, b, *_: (jnp.where(i == j, b, jnp.where(i < j, 0, parts - 1)), 0),
        )

    wide = 3 * D // 4
    return pl.pallas_call(
        functools.partial(project_kernel, len(pieces)),
        grid_spec=pltpu.PrefetchScalarGridSpec(
            num_scalar_prefetch=1,
            grid=(4, parts),
            in_specs=[x_spec(j) for j in range(4)]
            + [pl.BlockSpec((8, D), lambda i, b, *_: (0, 0))]
            + [pl.BlockSpec(memory_space=pl.ANY)] * len(pieces),
            out_specs=[
                pl.BlockSpec(
                    (step, D), lambda i, b, *_: (jnp.where(i == 0, b, parts - 1), 0)
                ),
                pl.BlockSpec((1, step, 2 * D), lambda i, b, *_: (i, b, 0)),
                pl.BlockSpec(memory_space=pl.ANY),
            ],
            scratch_shapes=[
                pltpu.VMEM((D, 3 * D), BF),
                pltpu.VMEM((4, D, wide), BF),
                pltpu.SemaphoreType.DMA((2,)),
            ],
        ),
        out_shape=[
            jax.ShapeDtypeStruct((tokens, D), BF),
            jax.ShapeDtypeStruct((4, tokens, 2 * D), BF),
            jax.ShapeDtypeStruct((D, 3 * D), BF),
        ],
        compiler_params=pltpu.CompilerParams(vmem_limit_bytes=40 * MIB),
        cost_estimate=pl.CostEstimate(
            flops=2 * tokens * D * 9 * D, bytes_accessed=30 * MIB, transcendentals=0
        ),
    )(table, *x_blocks, bias, *pieces)


def kv_specs(blocks, rows):
    return [
        pl.BlockSpec((1, 1, rows, 2 * D), functools.partial(lambda j, b, *_: (j, b, 0, 0), j))
        for j in range(blocks)
    ]


def attend_kernel(blocks, order_ref, len_ref, q_ref, *refs):
    kv_refs = refs[:blocks]
    prev_ref, ctx_ref, probs_ref, kv_all = refs[blocks:]
    rows = q_ref.shape[1]
    total = kv_all.shape[0]
    for j in range(blocks):
        start = pl.multiple_of(order_ref[j] * rows, rows)
        kv_all[pl.ds(start, rows), :] = kv_refs[j][0, 0]
    valid = len_ref[pl.program_id(0)]
    key_pos = lax.broadcasted_iota(jnp.int32, (1, total), 1)
    padding = jnp.where(key_pos < valid, 0.0, -1e9)
    for i in range(PAIRS):
        cols = slice(i * PAIR, (i + 1) * PAIR)
        vcols = slice(D + i * PAIR, D + (i + 1) * PAIR)
        query = stack_heads(q_ref[0, :, cols])
        raw = mm_nt(query, kv_all[:, cols])
        prev = prev_ref[0, 2 * i : 2 * i + 2].reshape(2 * rows, total).astype(F32)
        raw = raw + prev + padding
        largest = jnp.max(raw, -1, keepdims=True)
        expo = jnp.exp(raw - largest)
        summed = jnp.sum(expo, -1, keepdims=True)
        probs = (expo * (1.0 / summed)).astype(BF)
        probs_ref[0, 2 * i : 2 * i + 2] = probs.reshape(2, rows, total)
        ctx_ref[0, :, cols] = pick_heads(mm(probs, kv_all[:, vcols])).astype(BF)


def attend(order, lengths, queries, keys_values, prev_logits):
    seqs, rows, _ = queries.shape
    blocks = keys_values.shape[0]
    total = prev_logits.shape[-1]
    row_spec = lambda width: pl.BlockSpec((1, rows, width), lambda b, *_: (b, 0, 0))
    head_spec = pl.BlockSpec((1, HEADS, rows, total), lambda b, *_: (b, 0, 0, 0))
    return pl.pallas_call(
        functools.partial(attend_kernel, blocks),
        grid_spec=pltpu.PrefetchScalarGridSpec(
            num_scalar_prefetch=2,
            grid=(seqs,),
            in_specs=[row_spec(D)] + kv_specs(blocks, rows) + [head_spec],
            out_specs=[row_spec(D), head_spec],
            scratch_shapes=[pltpu.VMEM((total, 2 * D), BF)],
        ),
        out_shape=[
            jax.ShapeDtypeStruct(queries.shape, BF),
            jax.ShapeDtypeStruct(prev_logits.shape, BF),
        ],
        compiler_params=pltpu.CompilerParams(vmem_limit_bytes=48 * MIB),
        cost_estimate=pl.CostEstimate(
            flops=4 * seqs * HEADS * rows * total * PAIR,
            bytes_accessed=4 * seqs * HEADS * rows * total,
            transcendentals=seqs * HEADS * rows * total,
        ),
    )(order, lengths, queries, *[keys_values] * blocks, prev_logits)


def attend_back_kernel(blocks, order_ref, q_ref, *refs):
    kv_refs = refs[:blocks]
    probs_ref, dctx_ref, dlogits_ref, dq_ref = refs[blocks : blocks + 4]
    dkv_refs = refs[blocks + 4 : 2 * blocks + 4]
    kv_all, dkv_all = refs[2 * blocks + 4 :]
    rows = q_ref.shape[1]
    total = kv_all.shape[0]
    starts = [pl.multiple_of(order_ref[j] * rows, rows) for j in range(blocks)]
    for j in range(blocks):
        kv_all[pl.ds(starts[j], rows), :] = kv_refs[j][0, 0]
    for i in range(PAIRS):
        cols = slice(i * PAIR, (i + 1) * PAIR)
        vcols = slice(D + i * PAIR, D + (i + 1) * PAIR)
        query = stack_heads(q_ref[0, :, cols])
        dctx = stack_heads(dctx_ref[0, :, cols])
        probs = probs_ref[0, 2 * i : 2 * i + 2].reshape(2 * rows, total)
        dprobs = mm_nt(dctx, kv_all[:, vcols])
        wide = probs.astype(F32)
        prod = wide * dprobs
        weighted = jnp.sum(prod, -1, keepdims=True)
        dlogits = (prod - wide * weighted).astype(BF)
        dlogits_ref[0, 2 * i : 2 * i + 2] = dlogits.reshape(2, rows, total)
        dq_ref[0, :, cols] = (pick_heads(mm(dlogits, kv_all[:, cols])) * SCALE).astype(BF)
        dkv_all[:, cols] = mm_tn(dlogits, query).astype(BF)
        dkv_all[:, vcols] = mm_tn(probs, dctx).astype(BF)
    for j in range(blocks):
        dkv_refs[j][0] = dkv_all[pl.ds(starts[j], rows), :]


def attend_back(order, queries, keys_values, probs, dctx):
    seqs, rows, _ = queries.shape
    blocks = keys_values.shape[0]
    total = probs.shape[-1]
    row_spec = lambda width: pl.BlockSpec((1, rows, width), lambda b, *_: (b, 0, 0))
    head_spec = pl.BlockSpec((1, HEADS, rows, total), lambda b, *_: (b, 0, 0, 0))
    outs = pl.pallas_call(
        functools.partial(attend_back_kernel, blocks),
        grid_spec=pltpu.PrefetchScalarGridSpec(
            num_scalar_prefetch=1,
            grid=(seqs,),
            in_specs=[row_spec(D)] + kv_specs(blocks, rows) + [head_spec, row_spec(D)],
            out_specs=[head_spec, row_spec(D)] + [row_spec(2 * D)] * blocks,
            scratch_shapes=[pltpu.VMEM((total, 2 * D), BF), pltpu.VMEM((total, 2 * D), BF)],
        ),
        out_shape=[
            jax.ShapeDtypeStruct(probs.shape, BF),
            jax.ShapeDtypeStruct(queries.shape, BF),
        ]
        + [jax.ShapeDtypeStruct((seqs, rows, 2 * D), BF)] * blocks,
        compiler_params=pltpu.CompilerParams(vmem_limit_bytes=48 * MIB),
        cost_estimate=pl.CostEstimate(
            flops=8 * seqs * HEADS * rows * total * PAIR,
            bytes_accessed=4 * seqs * HEADS * rows * total,
            transcendentals=0,
        ),
    )(order, queries, *[keys_values] * blocks, probs, dctx)
    return outs[0], outs[1], outs[2:]


def gelu_and_slope(values):
    size = jnp.abs(values)
    bell = jnp.exp(values * values * -0.5)
    t = 1.0 / (1.0 + (0.3275911 * 0.7071067811865476) * size)
    tail = (0.5 * 1.061405429) * t + (0.5 * -1.453152027)
    tail = tail * t + (0.5 * 1.421413741)
    tail = tail * t + (0.5 * -0.284496736)
    tail = tail * t + (0.5 * 0.254829592)
    tail = tail * t * bell
    cdf = jnp.where(values >= 0.0, 1.0 - tail, tail)
    return values * cdf, cdf + values * bell * 0.3989422804014327


def norm(values):
    average = jnp.mean(values, -1, keepdims=True)
    centred = values - average
    inverse = lax.rsqrt(jnp.mean(centred * centred, -1, keepdims=True) + 1e-06)
    return centred * inverse, inverse


def norm_back(grad, normed, inverse):
    first = jnp.mean(grad, -1, keepdims=True)
    second = jnp.mean(grad * normed, -1, keepdims=True)
    return inverse * (grad - first - normed * second)


def load_middle(table_ref, in_refs, down_refs, w_out_ref, w_in_ref, w_down_ref, stage, sems):
    if len(in_refs) == 1:
        pltpu.make_async_copy(in_refs[0], w_in_ref, sems.at[1]).start()
        pltpu.make_async_copy(down_refs[0], w_down_ref, sems.at[2]).start()
        pltpu.make_async_copy(down_refs[1], w_out_ref, sems.at[0]).start()
        wait_whole(w_out_ref, sems.at[0])
    else:
        down = w_down_ref.shape[0] // 4
        wide = w_down_ref.shape[1] // 8
        high, half = D // 8, D // 16
        for piece, dp, seq in pieces_of(down_refs, table_ref):
            pltpu.make_async_copy(
                piece.at[pl.ds(down, half)], stage.at[seq, dp], sems.at[0]
            ).start()
        for piece, dp, seq in pieces_of(in_refs, table_ref):
            rows = pl.ds(pl.multiple_of(dp * high, high), high)
            cols = pl.ds(pl.multiple_of(seq * D, D), D)
            pltpu.make_async_copy(piece, w_in_ref.at[rows, cols], sems.at[1]).start()
        for piece, dp, seq in pieces_of(down_refs, table_ref):
            rows = pl.ds(pl.multiple_of(seq * down, down), down)
            cols = pl.ds(pl.multiple_of(dp * wide, wide), wide)
            pltpu.make_async_copy(
                piece.at[pl.ds(0, down)], w_down_ref.at[rows, cols], sems.at[2]
            ).start()
        wait_whole(stage, sems.at[0])
        for s in range(4):
            for d in range(8):
                cols = slice(s * down, (s + 1) * down)
                w_out_ref[d * high : d * high + half, cols] = stage[s, d][:, :down]
                w_out_ref[d * high + half : (d + 1) * high, cols] = stage[s, d][:, down:]


def middle_kernel(
    counts, table_ref, x_ref, ctx_ref, cot_ref, vec_ref, b_in_ref, *refs
):
    in_refs, refs = refs[: counts[0]], refs[counts[0] :]
    down_refs, refs = refs[: counts[1]], refs[counts[1] :]
    (
        out_ref, dh1_ref, dctx_ref, act_ref, dinner_ref, dbranch_ref, y1_ref, dattn_ref,
        dvec_ref, db_in_ref, w_out_ref, w_in_ref, w_down_ref, stage, sems,
    ) = refs

    @pl.when(pl.program_id(0) == 0)
    def _():
        load_middle(
            table_ref, in_refs, down_refs, w_out_ref, w_in_ref, w_down_ref, stage, sems
        )
        dvec_ref[...] = jnp.zeros_like(dvec_ref)
        db_in_ref[...] = jnp.zeros_like(db_in_ref)

    vec = lambda i: vec_ref[i : i + 1, :].astype(F32)
    total = lambda v: jnp.sum(v, 0, keepdims=True)
    h1 = x_ref[...].astype(F32) + (mm(ctx_ref[...], w_out_ref[...]) + vec(2))
    normed1, inverse1 = norm(h1)
    y1 = normed1 * vec(3) + vec(4)
    y1_low = y1.astype(BF)
    y1_ref[...] = y1_low

    @pl.when(pl.program_id(0) == 0)
    def _():
        wait_whole(w_in_ref, sems.at[1])

    inner = mm(y1_low, w_in_ref[...]) + b_in_ref[...].astype(F32)
    act, slope = gelu_and_slope(inner)
    act = act.astype(BF)
    act_ref[...] = act

    @pl.when(pl.program_id(0) == 0)
    def _():
        wait_whole(w_down_ref, sems.at[2])

    h2 = y1 + (mm_nt(act, w_down_ref[...]) + vec(5))
    normed2, inverse2 = norm(h2)
    out_ref[...] = (normed2 * vec(6) + vec(7)).astype(BF)
    cot = cot_ref[...].astype(F32)
    dh2 = norm_back(cot * vec(6), normed2, inverse2)
    dbranch = dh2.astype(BF)
    dbranch_ref[...] = dbranch
    dinner = (mm(dbranch, w_down_ref[...]) * slope).astype(BF)
    dinner_ref[...] = dinner
    dy1 = dh2 + mm_nt(dinner, w_in_ref[...])
    dh1 = norm_back(dy1 * vec(3), normed1, inverse1)
    dh1_ref[...] = dh1
    dattn = dh1.astype(BF)
    dattn_ref[...] = dattn
    dctx_ref[...] = mm_nt(dattn, w_out_ref[...]).astype(BF)
    db_in_ref[...] += total(dinner.astype(F32))
    dvec_ref[2:3, :] += total(dattn.astype(F32))
    dvec_ref[3:4, :] += total(dy1 * normed1)
    dvec_ref[4:5, :] += total(dy1)
    dvec_ref[5:6, :] += total(dbranch.astype(F32))
    dvec_ref[6:7, :] += total(cot * normed2)
    dvec_ref[7:8, :] += total(cot)


def middle(table, x, ctx, cot, vectors, b_in, in_pieces, down_pieces):
    tokens = x.shape[0]
    ff = b_in.shape[1]
    step = 256
    rows = lambda width: pl.BlockSpec((step, width), lambda i, *_: (i, 0))
    whole = lambda a: pl.BlockSpec(a.shape, lambda i, *_: (0, 0))
    fixed = lambda *shape: pl.BlockSpec(shape, lambda i, *_: (0, 0))
    sds = jax.ShapeDtypeStruct
    counts = (len(in_pieces), len(down_pieces))
    return pl.pallas_call(
        functools.partial(middle_kernel, counts),
        grid_spec=pltpu.PrefetchScalarGridSpec(
            num_scalar_prefetch=1,
            grid=(tokens // step,),
            in_specs=[rows(D)] * 3
            + [whole(vectors), whole(b_in)]
            + [pl.BlockSpec(memory_space=pl.ANY)] * sum(counts),
            out_specs=[rows(D)] * 3
            + [rows(ff)] * 2
            + [rows(D)] * 3
            + [fixed(8, D), fixed(1, ff)],
            scratch_shapes=[
                pltpu.VMEM((D, D), BF),
                pltpu.VMEM((D, ff), BF),
                pltpu.VMEM((D, ff), BF),
                pltpu.VMEM((4, 8, D // 16, ff // 8), BF),
                pltpu.SemaphoreType.DMA((3,)),
            ],
        ),
        out_shape=[
            sds((tokens, D), BF),
            sds((tokens, D), F32),
            sds((tokens, D), BF),
            sds((tokens, ff), BF),
            sds((tokens, ff), BF),
            sds((tokens, D), BF),
            sds((tokens, D), BF),
            sds((tokens, D), BF),
            sds((8, D), F32),
            sds((1, ff), F32),
        ],
        compiler_params=pltpu.CompilerParams(vmem_limit_bytes=56 * MIB),
        cost_estimate=pl.CostEstimate(
            flops=tokens * (8 * D * ff + 4 * D * D),
            bytes_accessed=40 * MIB,
            transcendentals=2 * tokens * ff,
        ),
    )(table, x, ctx, cot, vectors, b_in, *in_pieces, *down_pieces)


def grad_in_kernel(where_ref, y1_ref, dinner_ref, send_ref, keep_ref):
    z, y = where_ref[0], where_ref[1]
    step = pl.program_id(0)
    high = D // 8
    grad = mm_tn(y1_ref[...], dinner_ref[...]).astype(BF)
    for d in range(8):
        rows = grad[d * high : (d + 1) * high]
        far_y, far_z = y ^ (d & 1), ((d >> 1) - z) & 3

        @pl.when(step < 2)
        def _():
            send_ref[far_y, 0, far_z] = rows

        @pl.when(step >= 2)
        def _():
            keep_ref[far_y, 0, far_z] = rows


def grad_in(where, y1, dinner):
    tokens, ff = dinner.shape
    wide = ff // 4

    def columns(t, where):
        return (0, 2 * (where[2] ^ (t & 1)) + (where[3] ^ (1 - (t >> 1))))

    piece = (2, 1, 4, D // 8, wide)
    shape = jax.ShapeDtypeStruct((2, 2, 4, D // 8, wide), BF)
    return pl.pallas_call(
        grad_in_kernel,
        grid_spec=pltpu.PrefetchScalarGridSpec(
            num_scalar_prefetch=1,
            grid=(4,),
            in_specs=[
                pl.BlockSpec((tokens, D), lambda t, w: (0, 0)),
                pl.BlockSpec((tokens, wide), columns),
            ],
            out_specs=[
                pl.BlockSpec(piece, lambda t, w: (0, jnp.minimum(t, 1), 0, 0, 0)),
                pl.BlockSpec(piece, lambda t, w: (0, jnp.maximum(t - 2, 0), 0, 0, 0)),
            ],
        ),
        out_shape=[shape, shape],
        compiler_params=pltpu.CompilerParams(vmem_limit_bytes=40 * MIB),
        cost_estimate=pl.CostEstimate(
            flops=2 * tokens * D * ff, bytes_accessed=14 * MIB, transcendentals=0
        ),
    )(where, y1, dinner)


def grad_down_kernel(
    where_ref, dbranch_ref, act_ref, ctx_ref, dattn_ref, send_ref, keep_ref, grad_out
):
    y, x, core = where_ref[1], where_ref[2], where_ref[3]
    step = pl.program_id(0)
    wide, down = D // 2, D // 4
    high, half = D // 8, D // 16

    @pl.when(step == 0)
    def _():
        grad_out[...] = mm_tn(ctx_ref[...], dattn_ref[...])

    def put(far_x, far_y, rows, cols, even, odd):
        first = core == 0
        keep_ref[far_x, far_y, 0, rows, cols] = jnp.where(first, even, odd).astype(BF)
        send_ref[far_x, far_y, 0, rows, cols] = jnp.where(first, odd, even).astype(BF)

    grad = mm_tn(dbranch_ref[...], act_ref[...])
    for j in range(2):
        top = pl.multiple_of((2 * step + j) * high, high)
        upper, lower = grad_out[pl.ds(top, half), :], grad_out[pl.ds(top + half, half), :]
        for i in range(2):
            pair = [slice((2 * i + k) * down, (2 * i + k + 1) * down) for k in range(2)]
            side = slice(j * wide, (j + 1) * wide)
            far = (x ^ i, y ^ j)
            put(*far, slice(0, down), slice(None), grad[pair[0], side], grad[pair[1], side])
            tail = slice(down, down + half)
            put(*far, tail, slice(0, down), upper[:, pair[0]], upper[:, pair[1]])
            put(*far, tail, slice(down, 2 * down), lower[:, pair[0]], lower[:, pair[1]])


def grad_down(where, dbranch, act, ctx, dattn):
    tokens, ff = act.shape
    wide = ff // 4
    whole = pl.BlockSpec((tokens, D), lambda t, w: (0, 0))
    piece = (D // 4 + D // 16, ff // 8)
    spec = pl.BlockSpec((2, 2, 1) + piece, lambda t, w: (0, 0, (t - w[0]) & 3, 0, 0))
    shape = jax.ShapeDtypeStruct((2, 2, 4) + piece, BF)
    return pl.pallas_call(
        grad_down_kernel,
        grid_spec=pltpu.PrefetchScalarGridSpec(
            num_scalar_prefetch=1,
            grid=(4,),
            in_specs=[whole, pl.BlockSpec((tokens, wide), lambda t, w: (0, t)), whole, whole],
            out_specs=[spec, spec],
            scratch_shapes=[pltpu.VMEM((D, D), F32)],
        ),
        out_shape=[shape, shape],
        compiler_params=pltpu.CompilerParams(vmem_limit_bytes=40 * MIB),
        cost_estimate=pl.CostEstimate(
            flops=2 * tokens * D * (ff + D), bytes_accessed=20 * MIB, transcendentals=0
        ),
    )(where, dbranch, act, ctx, dattn)


def grad_qkv_kernel(
    where_ref, x0_ref, x2_ref, dq_ref, dkv0_ref, dkv2_ref, send_ref, keep_ref, grad
):
    z, y, x, core = (where_ref[i] for i in range(4))
    step = pl.program_id(0)
    wide, high = 3 * D // 4, D // 8

    @pl.when(step == 0)
    def _():
        grad[:, :D] = mm_tn(x0_ref[...], dq_ref[...])

    for t in (1, 2):

        @pl.when(step == t)
        def _():
            grad[:, t * D : (t + 1) * D] = mm_tn(x0_ref[...], dkv0_ref[...]) + mm_tn(
                x2_ref[...], dkv2_ref[...]
            )

    @pl.when(step == 2)
    def _():
        first = core == 0
        for i in range(2):
            even = grad[:, 2 * i * wide : (2 * i + 1) * wide]
            odd = grad[:, (2 * i + 1) * wide : (2 * i + 2) * wide]
            kept = jnp.where(first, even, odd).astype(BF)
            sent = jnp.where(first, odd, even).astype(BF)
            for d in range(8):
                rows = slice(d * high, (d + 1) * high)
                far = (y ^ (d & 1), x ^ i, ((d >> 1) - z) & 3)
                keep_ref[far] = kept[rows]
                send_ref[far] = sent[rows]


def grad_qkv(where, x0, x2, dq, dkv0, dkv2):
    tokens = x0.shape[0]
    whole = pl.BlockSpec((tokens, D), lambda t, w: (0, 0))
    part = pl.BlockSpec((tokens, D), lambda t, w: (0, jnp.maximum(t - 1, 0)))
    dims = (2, 2, 4, D // 8, 3 * D // 4)
    spec = pl.BlockSpec(dims, lambda t, w: (0, 0, 0, 0, 0))
    shape = jax.ShapeDtypeStruct(dims, BF)
    return pl.pallas_call(
        grad_qkv_kernel,
        grid_spec=pltpu.PrefetchScalarGridSpec(
            num_scalar_prefetch=1,
            grid=(3,),
            in_specs=[whole, whole, whole, part, part],
            out_specs=[spec, spec],
            scratch_shapes=[pltpu.VMEM((D, 3 * D), F32)],
        ),
        out_shape=[shape, shape],
        compiler_params=pltpu.CompilerParams(vmem_limit_bytes=48 * MIB),
        cost_estimate=pl.CostEstimate(
            flops=2 * tokens * D * 5 * D, bytes_accessed=16 * MIB, transcendentals=0
        ),
    )(where, x0, x2, dq, dkv0, dkv2)


def grad_rows_kernel(own, *refs):
    if own:
        dkv_ref, got_ref, w_ref, dq_ref, dh1_ref, dx_ref, sum_ref, bias_ref = refs
    else:
        dkv_ref, got_ref, w_ref, dx_ref, sum_ref, bias_ref = refs

    @pl.when(pl.program_id(0) == 0)
    def _():
        bias_ref[...] = jnp.zeros_like(bias_ref)

    total = (dkv_ref[...].astype(F32) + got_ref[...].astype(F32)).astype(BF)
    sum_ref[...] = total
    bias_ref[1:2, :] += jnp.sum(total[:, D:].astype(F32), 0, keepdims=True)
    dx = mm_nt(total, w_ref[:, D:])
    if own:
        dq = dq_ref[...]
        bias_ref[0:1, :] += jnp.sum(dq.astype(F32), 0, keepdims=True)
        dx = dx + mm_nt(dq, w_ref[:, :D]) + dh1_ref[...]
    dx_ref[...] = dx.astype(dx_ref.dtype)


def grad_rows(dkv, got, w_qkv, dq=None, dh1=None):
    own = dq is not None
    tokens = dkv.shape[0]
    step = 512
    rows = lambda width: pl.BlockSpec((step, width), lambda i: (i, 0))
    sds = jax.ShapeDtypeStruct
    return pl.pallas_call(
        functools.partial(grad_rows_kernel, own),
        grid=(tokens // step,),
        in_specs=[
            rows(2 * D),
            rows(2 * D),
            pl.BlockSpec((D, 3 * D), lambda i: (0, 0), pipeline_mode=pl.Buffered(1)),
        ]
        + [rows(D)] * (2 if own else 0),
        out_specs=[rows(D), rows(2 * D), pl.BlockSpec((8, D), lambda i: (0, 0))],
        out_shape=[
            sds((tokens, D), F32 if own else BF),
            sds((tokens, 2 * D), BF),
            sds((8, D), F32),
        ],
        compiler_params=pltpu.CompilerParams(vmem_limit_bytes=40 * MIB),
        cost_estimate=pl.CostEstimate(
            flops=2 * tokens * D * (3 if own else 2) * D,
            bytes_accessed=16 * MIB,
            transcendentals=0,
        ),
    )(dkv, got, w_qkv, *((dq, dh1) if own else ()))


def gather_small(b_in, vectors):
    dp, seq = lax.axis_size("dp"), lax.axis_size("seq")
    small = jnp.concatenate([vectors.reshape(-1), b_in])
    whole = lax.all_gather(small, BOTH, axis=0, tiled=False)
    nv = vectors.size
    vec = whole[:, :nv].reshape((dp, seq) + vectors.shape).transpose(1, 2, 0, 3)
    return whole[:, nv:].reshape(1, -1), vec.reshape(8, D)


def reduce_small(g_b, g_vec):
    dp, seq = lax.axis_size("dp"), lax.axis_size("seq")
    vec = g_vec.reshape(seq, 8 // seq, dp, D // dp).transpose(2, 0, 1, 3)
    small = jnp.concatenate([vec.reshape(dp * seq, -1), g_b.reshape(dp * seq, -1)], 1)
    mine = lax.psum_scatter(small, BOTH, scatter_dimension=0, tiled=True)[0]
    nv = 8 * D // (dp * seq)
    return mine[nv:], mine[:nv].reshape(8 // seq, D // dp)


def gather_plain(w_qkv, w_out, w_in, w_down_t):
    both = lambda a, first, second: lax.all_gather(
        lax.all_gather(a, first, axis=0, tiled=True), second, axis=1, tiled=True
    )
    return (
        [both(w_qkv, "dp", "seq")],
        [both(w_in, "dp", "seq")],
        [both(w_down_t, "seq", "dp"), both(w_out, "dp", "seq")],
    )


def reduce_plain(a, first, second):
    part = lax.psum_scatter(a.astype(BF), first, scatter_dimension=0, tiled=True)
    return lax.psum_scatter(part, second, scatter_dimension=1, tiled=True).astype(F32)


def shards(
    hidden_states, prev_logits, lengths, w_qkv, w_out, w_in, w_down, b_in, vectors, cotangent
):
    seqs, rows, _ = hidden_states.shape
    tokens = seqs * rows
    seq = lax.axis_size("seq")
    me = lax.axis_index("seq")
    apart = by_pieces()
    order = jnp.arange(seq, dtype=jnp.int32) ^ me
    x0 = hidden_states.reshape(tokens, D)
    x2 = swap_x(x0)
    x_blocks = [x0, swap_core(x0), x2, swap_core(x2)]
    f_b, f_vec = gather_small(b_in, vectors)
    if apart:
        table, where = piece_table(), jnp.stack(place()).astype(jnp.int32)
        half = w_out.shape[0] // 2
        low_rows = jnp.concatenate([w_out[:half], w_out[half:]], 1)
        qkv_pieces = gather_pieces(w_qkv)
        in_pieces = gather_pieces(w_in)
        down_pieces = gather_pieces(jnp.concatenate([w_down.T, low_rows], 0))
    else:
        table = jnp.zeros((2,), jnp.int32)
        qkv_pieces, in_pieces, down_pieces = gather_plain(w_qkv, w_out, w_in, w_down.T)
    queries, keys_values, f_qkv = project(table, x_blocks, f_vec.astype(F32), qkv_pieces)
    queries = queries.reshape(seqs, rows, D)
    keys_values = keys_values.reshape(seq, seqs, rows, 2 * D)
    ctx, probs = attend(order, lengths, queries, keys_values, prev_logits)
    ctx = ctx.reshape(tokens, D)
    out, dh1, dctx, act, dinner, dbranch, y1, dattn, dvec, db_in = middle(
        table, x0, ctx, cotangent.reshape(tokens, D), f_vec, f_b, in_pieces, down_pieces
    )
    if apart:
        o_in = reduce_pieces(*grad_in(where, y1, dinner), swap_y, swap_x)
        o_low = reduce_pieces(*grad_down(where, dbranch, act, ctx, dattn), swap_x, swap_y)
        down = w_down.shape[1]
        o_down = o_low[:down].T
        o_out = jnp.concatenate([o_low[down:, :down], o_low[down:, down:]], 0)
    else:
        o_in = reduce_plain(mm_tn(y1, dinner), "dp", "seq")
        o_down = reduce_plain(mm_tn(act, dbranch), "dp", "seq")
        o_out = reduce_plain(mm_tn(ctx, dattn), "dp", "seq")
    dlogits, dq, dkv = attend_back(
        order, queries, keys_values, probs, dctx.reshape(seqs, rows, D)
    )
    dq = dq.reshape(tokens, D)
    dkv = [b.reshape(tokens, 2 * D) for b in dkv]
    dx2, dkv2, bias2 = grad_rows(dkv[2], swap_core(dkv[3]), f_qkv)
    got_rows = swap_x(dx2)
    dx0, dkv0, bias0 = grad_rows(dkv[0], swap_core(dkv[1]), f_qkv, dq, dh1)
    if apart:
        o_qkv = reduce_pieces(*grad_qkv(where, x0, x2, dq, dkv0, dkv2), swap_y, swap_x)
    else:
        g_kv = mm_tn(x0, dkv0) + mm_tn(x2, dkv2)
        o_qkv = reduce_plain(jnp.concatenate([mm_tn(x0, dq), g_kv], 1), "dp", "seq")
    g_b, g_vec = reduce_small(db_in, dvec + bias0 + bias2)
    grad_hidden = low(dx0 + got_rows.astype(F32))
    shape = hidden_states.shape
    return (
        out.reshape(shape),
        grad_hidden.reshape(shape),
        dlogits,
        o_qkv,
        o_out,
        o_in,
        o_down,
        g_b,
        g_vec,
    )


def solution(mesh):
    return jax.shard_map(
        shards,
        mesh=mesh,
        in_specs=(
            P("dp", "seq", None),
            P("dp", None, "seq", None),
            P("dp"),
            P("dp", "seq"),
            P("dp", "seq"),
            P("dp", "seq"),
            P("dp", "seq"),
            P(("dp", "seq")),
            P("seq", "dp"),
            P("dp", "seq", None),
        ),
        out_specs=(
            P("dp", "seq", None),
            P("dp", "seq", None),
            P("dp", None, "seq", None),
            P("dp", "seq"),
            P("dp", "seq"),
            P("dp", "seq"),
            P("dp", "seq"),
            P(("dp", "seq")),
            P("seq", "dp"),
        ),
        check_vma=False,
    )
```

time: 633 us -> 520 us (0.82)
  waiting for transfers between devices: 284 us -> 107 us
  blocking collectives: 0 us -> 111 us
  local copies, waits for them, and re-layouts: 115 us -> 30 us
  matrix products: 82.9 us -> 0 us
  Pallas kernels: 102 us -> 170 us
  starting transfers between devices: 5.17 us -> 64.3 us
  between operations: 14.8 us -> 1.39 us
  other arithmetic: 24.8 us -> 31.6 us
    all_gather x1 -> x0, waiting for transfers between devices: 131 us -> none  [gather_weights(): lax.all_gather(packed, BOTH, axis=0, tiled=False).reshape(dp, seq, -1, D)]
    unnamed x0 -> x2, blocking collectives: none -> 111 us
    dot_general x18 -> x0, matrix products: 82.9 us -> none  [the longest x8 41.6 us: mm_tn(): lax.dot_general(a, b, (((0,), (0,)), ((), ())), preferred_element_type=F32)]
    reduce_scatter x1 -> x0, waiting for transfers between devices: 74.6 us -> none  [reduce_grads(): lax.psum_scatter(packed.reshape(dp * seq, -1, D), BOTH, scatter_dimension...]
    pallas_call x1 -> x7, Pallas kernels: 44 us -> 112 us  [the longest x1 48.4 us: middle(): pl.pallas_call(functools.partial(middle_kernel, counts), grid_spec=pltpu....]
    ppermute x6 -> x54, starting transfers between devices: 5.09 us -> 64.3 us  [the longest x18 36.9 us: shift_z(): lax.ppermute(a, 'dp', [(i, (i + 2 * places) % size) for i in range(size)])]
    reshape x19 -> x9, local copies, waits for them, and re-layouts: 36.2 us -> 1.85 us  [the longest x2 0.78 us: gather_small(): return (whole[:, nv:].reshape(1, -1), vec.reshape(8, D))]
    ppermute x6 -> x54, waiting for transfers between devices: 78.9 us -> 107 us  [the longest x36 72.3 us: swap(): return lax.ppermute(a, axis, [(i, i ^ bit) for i in range(size)])]
  transfers between devices with their start and end apart: 8 -> 54, of which waited for: 4 -> 19; matrix products, arithmetic and copies ran while one was open for 13% -> 6% of each run, Pallas kernels for 0% -> 17%
where the time goes in v2:
time: 520 us; the launch traced here: 516 us
  Pallas kernels  170 us (33%)
  blocking collectives  111 us (21%)
  waiting for transfers between devices  107 us (21%)
  starting transfers between devices  64.3 us (12%)
  other arithmetic  31.6 us (6%)
  local copies, waits for them, and re-layouts  30 us (6%)
    unnamed x2, blocking collectives  111 us
    ppermute x36, waiting for transfers between devices, swap(): return lax.ppermute(a, axis, [(i, i ^ bit) for i in range(size)])  72.3 us
    pallas_call x1, Pallas kernels, middle(): pl.pallas_call(functools.partial(middle_kernel, counts), grid_spec=pltpu....  48.4 us
    ppermute x18, starting transfers between devices, shift_z(): lax.ppermute(a, 'dp', [(i, (i + 2 * places) % size) for i in range(size)])  36.9 us
    ppermute x18, waiting for transfers between devices, shift_z(): lax.ppermute(a, 'dp', [(i, (i + 2 * places) % size) for i in range(size)])  34.9 us
    pallas_call x1, Pallas kernels, attend_back(): pl.pallas_call(functools.partial(attend_back_kernel, blocks), grid_spec=p...  31.6 us
    ppermute x36, starting transfers between devices, swap(): return lax.ppermute(a, axis, [(i, i ^ bit) for i in range(size)])  27.4 us
    pallas_call x1, Pallas kernels, attend(): pl.pallas_call(functools.partial(attend_kernel, blocks), grid_spec=pltpu....  26.3 us
  transfers between devices with their start and end apart: 54, of which 19 were waited for; matrix products, arithmetic and copies ran while one was open for 6% of the time, Pallas kernels for 17%

profile of v2, /device:TPU:0, one launch (start us, length us, event | category | flops | bytes accessed | tf_op | source)
XLA Modules:
  0.0 515.9 jit_solution(5382530741149927947)
XLA Ops:
  0.7 3.1 collective-permute-start.3
  10.6 3.8 collective-permute-start.15
  14.4 6.1 %collective-permute-done.4 = bf16[96,576]{1,0:T(8,128)(2,1)S(1)} collective-permute-done((bf16[96,576]{1,0:T(8,128)(2,1)}, bf16[96,576]{1,0:T(8,128)(2,1)S(1)}, u32[]{:S(2)}, u32[]{:S(2)}) %collective-permute-start.4) | collective-permute-done | bytes 110624 | tf_op jit(solution)/shard_map/ppermute | solution.py:67
  22.7 2.9 collective-permute-start.14
  25.7 9.5 %collective-permute-start.23 = (bf16[240,384]{1,0:T(8,128)(2,1)S(1)}, bf16[240,384]{1,0:T(8,128)(2,1)S(1)}, u32[]{:S(2)}, u32[]{:S(2)}) collective-permute-start(bf16[240,384]{1,0:T(8,128)(2,1)S(1)} %maximum_maximum_fusion), channel_id=1, source_target_pairs={{0,8},{4,12},{8,16},{12,20},{16,24},{20,28},{24,0},{28,4},{1,9},{5... | collective-permute-start | bytes 552968 | tf_op jit(solution)/shard_map/ppermute | solution.py:67
  35.2 6.5 %collective-permute-done.14 = bf16[96,768]{1,0:T(8,128)(2,1)S(1)} collective-permute-done((bf16[96,768]{1,0:T(8,128)(2,1)}, bf16[96,768]{1,0:T(8,128)(2,1)S(1)}, u32[]{:S(2)}, u32[]{:S(2)}) %collective-permute-start.14) | collective-permute-done | bytes 147488 | tf_op jit(solution)/shard_map/ppermute | solution.py:67
  50.1 5.7 %collective-permute-done.7.refs_2_ = bf16[4,96,576]{2,1,0:T(8,128)(2,1)S(1)} collective-permute-done((bf16[4,96,576]{2,1,0:T(8,128)(2,1)S(1)}, bf16[4,96,576]{2,1,0:T(8,128)(2,1)S(1)}, u32[]{:S(2)}, u32[]{:S(2)}) %collective-permute-start.7) | collective-permute-done | bytes 442400 | tf_op jit(solution)/shard_map/ppermute | solution.py:50
  58.9 9.6 %collective-permute-done.17.refs_2_ = bf16[4,96,768]{2,1,0:T(8,128)(2,1)S(1)} collective-permute-done((bf16[4,96,768]{2,1,0:T(8,128)(2,1)S(1)}, bf16[4,96,768]{2,1,0:T(8,128)(2,1)S(1)}, u32[]{:S(2)}, u32[]{:S(2)}) %collective-permute-start.17) | collective-permute-done | bytes 589856 | tf_op jit(solution)/shard_map/ppermute | solution.py:50
  73.1 10.4 %collective-permute-done.27.refs_10_ = bf16[4,240,384]{2,1,0:T(8,128)(2,1)} collective-permute-done((bf16[4,240,384]{2,1,0:T(8,128)(2,1)S(1)}, bf16[4,240,384]{2,1,0:T(8,128)(2,1)}, u32[]{:S(2)}, u32[]{:S(2)}) %collective-permute-start.27) | collective-permute-done | bytes 737312 | tf_op jit(solution)/shard_map/ppermute | solution.py:50
  83.5 3.9 collective-permute-done.26.refs_9_
  91.8 9.9 %collective-permute-done.8.refs_3_ = bf16[4,96,576]{2,1,0:T(8,128)(2,1)} collective-permute-done((bf16[4,96,576]{2,1,0:T(8,128)(2,1)S(1)}, bf16[4,96,576]{2,1,0:T(8,128)(2,1)}, u32[]{:S(2)}, u32[]{:S(2)}) %collective-permute-start.8) | collective-permute-done | bytes 442400 | tf_op jit(solution)/shard_map/ppermute | solution.py:50
  104.5 56.8 %all-reduce = bf16[9216]{0:T(1024)(128)(2,1)S(1)} all-reduce(bf16[9216]{0:T(1024)(128)(2,1)S(1)} %dynamic-update-slice), channel_id=2, replica_groups=mesh['dp'=8,'seq'=4] {'dp','seq'}, use_global_device_ids=true, to_apply=%add | all-reduce | flops 9216 | bytes 36864
  166.8 23.4 %shard_map.169 = (bf16[1024,768]{1,0:T(8,128)(2,1)S(1)}, bf16[4,1024,1536]{2,1,0:T(8,128)(2,1)}, bf16[768,2304]{1,0:T(8,128)(2,1)}) custom-call(s32[64]{0:T(128)S(1)} %stack.78.table_ref, bf16[1024,768]{1,0:T(8,128)(2,1)S(1)} %bitcast.234, bf16[1024,768]{1,0:T(8,128)(2,1)} %collective-permute-done.x1_ref, bf16[1024,768]{1,0:T(8,128)(2,1)} %collective-permute-done.1.x2_ref, ...), custom_call_target="tpu_custom_call" | custom-call | flops 10871635968 | bytes 31457280 | tf_op jit(solution)/shard_map/pallas_call | solution.py:174
  190.2 26.3 %shard_map.170 = (bf16[8,128,768]{2,1,0:T(8,128)(2,1)S(1)}, bf16[8,12,128,512]{3,2,1,0:T(8,128)(2,1)}) custom-call(s32[4]{0:T(128)S(1)} %iota_xor_fusion.order_ref, s32[8]{0:T(128)S(1)} %copy-done.13, bf16[8,128,768]{2,1,0:T(8,128)(2,1)S(1)} %bitcast.224, bf16[4,8,128,1536]{3,2,1,0:T(8,128)(2,1)} %bitcast.238, bf16[4,8,128,1536]{3,2,1,0:T(8,128)(2,1)} %bitcast.239, ...), custom_call_target="tpu_custom_call" | custom-call | flops 3221225472 | bytes 25165824 | tf_op jit(solution)/shard_map/pallas_call | solution.py:246
  219.6 48.4 %shard_map.171 = (bf16[1024,768]{1,0:T(8,128)(2,1)}, f32[1024,768]{1,0:T(8,128)}, bf16[1024,768]{1,0:T(8,128)(2,1)}, bf16[1024,3072]{1,0:T(8,128)(2,1)}, bf16[10...) custom-call(s32[64]{0:T(128)} %copy-done.12, ...), custom_call_target="tpu_custom_call" | custom-call | flops 21743271936 | bytes 41943040 | tf_op jit(solution)/shard_map/pallas_call | solution.py:457
  269.4 31.6 %shard_map.172 = (bf16[8,12,128,512]{3,2,1,0:T(8,128)(2,1)}, bf16[8,128,768]{2,1,0:T(8,128)(2,1)S(1)}, bf16[8,128,1536]{2,1,0:T(8,128)(2,1)}, bf16[8,128,1536]{2...) custom-call(s32[4]{0:T(128)S(1)} %iota_xor_fusion.order_ref, ...), custom_call_target="tpu_custom_call" | custom-call | flops 6442450944 | bytes 25165824 | tf_op jit(solution)/shard_map/pallas_call | solution.py:303
  304.1 10.1 %shard_map.176 = (bf16[2,2,4,240,384]{4,3,2,1,0:T(8,128)(2,1)S(1)}, bf16[2,2,4,240,384]{4,3,2,1,0:T(8,128)(2,1)S(1)}) custom-call(s32[4]{0:T(128)S(1)} %pad_add_fusion.where_ref, bf16[1024,768]{1,0:T(8,128)(2,1)S(1)} %copy-done.29, bf16[1024,3072]{1,0:T(8,128)(2,1)} %get-tuple-element.63.act_ref, bf16[1024,768]{1,0:T(8,128)(2,1)S(1)} %bitcast.237, ...), custom_call_target="tpu_custom_call" | custom-call | flops 6039797760 | bytes 20971520 | tf_op jit(solution)/shard_map/pallas_call | solution.py:585
  314.3 2.8 copy-done.27
  317.1 7.8 %shard_map.177 = (bf16[2,2,4,96,768]{4,3,2,1,0:T(8,128)(2,1)S(1)}, bf16[2,2,4,96,768]{4,3,2,1,0:T(8,128)(2,1)S(1)}) custom-call(s32[4]{0:T(128)S(1)} %pad_add_fusion.where_ref, bf16[1024,768]{1,0:T(8,128)(2,1)S(1)} %copy-done.28, bf16[1024,3072]{1,0:T(8,128)(2,1)S(1)} %copy-done.27), custom_call_target="tpu_custom_call" | custom-call | flops 4831838208 | bytes 14680064 | tf_op jit(solution)/shard_map/pallas_call | solution.py:525
  325.5 6.6 %collective-permute-done.48 = bf16[2,2,4,96,768]{4,3,2,1,0:T(8,128)(2,1)} collective-permute-done((bf16[2,2,4,96,768]{4,3,2,1,0:T(8,128)(2,1)S(1)}, bf16[2,2,4,96,768]{4,3,2,1,0:T(8,128)(2,1)}, u32[]{:S(2)}, u32[]{:S(2)}) %collective-permute-start.48) | collective-permute-done | bytes 2359328 | tf_op jit(solution)/shard_map/ppermute | solution.py:50
  337.1 3.0 fusion
  344.3 3.0 shard_map.174
  351.0 6.7 %shard_map.173 = (f32[1024,768]{1,0:T(8,128)S(1)}, bf16[1024,1536]{1,0:T(8,128)(2,1)S(1)}, f32[8,768]{1,0:T(8,128)S(1)}) custom-call(bf16[1024,1536]{1,0:T(8,128)(2,1)S(1)} %bitcast.226, bf16[1024,1536]{1,0:T(8,128)(2,1)S(1)} %collective-permute-done.33.refs_1_, bf16[768,2304]{1,0:T(8,128)(2,1)} %get-tuple-element.50.refs_2_, ...), custom_call_target="tpu_custom_call" | custom-call | flops 3623878656 | bytes 16777216 | tf_op jit(solution)/shard_map/pallas_call | solution.py:687
  359.5 12.7 %shard_map.175 = (bf16[2,2,4,96,576]{4,3,2,1,0:T(8,128)(2,1)}, bf16[2,2,4,96,576]{4,3,2,1,0:T(8,128)(2,1)}) custom-call(s32[4]{0:T(128)S(1)} %pad_add_fusion.where_ref, bf16[1024,768]{1,0:T(8,128)(2,1)S(1)} %bitcast.235, bf16[1024,768]{1,0:T(8,128)(2,1)} %collective-permute-done.1.x2_ref, bf16[1024,768]{1,0:T(8,128)(2,1)S(1)} %bitcast.229, ...), custom_call_target="tpu_custom_call" | custom-call | flops 6039797760 | bytes 16777216 | tf_op jit(solution)/shard_map/pallas_call | solution.py:643
  378.3 12.9 %collective-permute-done.50 = bf16[4,96,768]{2,1,0:T(8,128)(2,1)} collective-permute-done((bf16[4,96,768]{2,1,0:T(8,128)(2,1)}, bf16[4,96,768]{2,1,0:T(8,128)(2,1)}, u32[]{:S(2)}, u32[]{:S(2)}) %collective-permute-start.50) | collective-permute-done | bytes 589856 | tf_op jit(solution)/shard_map/ppermute | solution.py:50
  403.2 54.6 %all-reduce.1 = f32[32,288]{1,0:T(8,128)S(1)} all-reduce(f32[32,288]{1,0:T(8,128)S(1)} %pad_maximum_fusion.4), channel_id=3, replica_groups=mesh['dp'=8,'seq'=4] {'dp','seq'}, use_global_device_ids=true, to_apply=%region_0.0.clone | all-reduce | flops 9216 | bytes 73728
  471.3 3.1 add_convert_fusion
  477.1 7.9 %collective-permute-done.46 = bf16[240,384]{1,0:T(8,128)(2,1)S(1)} collective-permute-done((bf16[240,384]{1,0:T(8,128)(2,1)S(1)}, bf16[240,384]{1,0:T(8,128)(2,1)S(1)}, u32[]{:S(2)}, u32[]{:S(2)}) %collective-permute-start.46) | collective-permute-done | bytes 184352 | tf_op jit(solution)/shard_map/ppermute | solution.py:67
  490.0 10.3 %collective-permute-done.38 = bf16[4,96,576]{2,1,0:T(8,128)(2,1)S(1)} collective-permute-done((bf16[4,96,576]{2,1,0:T(8,128)(2,1)S(1)}, bf16[4,96,576]{2,1,0:T(8,128)(2,1)S(1)}, u32[]{:S(2)}, u32[]{:S(2)}) %collective-permute-start.38) | collective-permute-done | bytes 442400 | tf_op jit(solution)/shard_map/ppermute | solution.py:50
  501.6 3.8 collective-permute-start.41
  506.0 3.7 collective-permute-done.39
  509.7 4.2 collective-permute-done.40
  (229 shorter events, 103.4 us)
Async XLA Ops:
  8.3 64.2 %collective-permute-start.1 = (bf16[1024,768]{1,0:T(8,128)(2,1)}, bf16[1024,768]{1,0:T(8,128)(2,1)}, u32[]{:S(2)}, u32[]{:S(2)}) collective-permute-start(bf16[1024,768]{1,0:T(8,128)(2,1)} %bitcast.231), channel_id=1, source_target_pairs={{0,2},{1,3},{2,0},{3,1},{4,6},{5,7},{6,4},{7,5},{8,10},{9,11},{10,... | collective-permute-start | bytes 4718600 | tf_op jit(solution)/shard_map/ppermute | solution.py:50
  21.6 26.7 %collective-permute-start.9 = (bf16[4,96,576]{2,1,0:T(8,128)(2,1)S(1)}, bf16[4,96,576]{2,1,0:T(8,128)(2,1)S(1)}, u32[]{:S(2)}, u32[]{:S(2)}) collective-permute-start(bf16[4,96,576]{2,1,0:T(8,128)(2,1)S(1)} %pad_maximum_fusion.2.refs_0_), channel_id=1, source_target_pairs={{0,1},{1,0},{2,3},{3,2},{4,5},{5,4},{6,7},{7,6},{8,9},{9,8},{10,11... | collective-permute-start | bytes 1327112 | tf_op jit(solution)/shard_map/ppermute | solution.py:50
  22.7 19.0 %collective-permute-start.24 = (bf16[240,384]{1,0:T(8,128)(2,1)S(1)}, bf16[240,384]{1,0:T(8,128)(2,1)S(1)}, u32[]{:S(2)}, u32[]{:S(2)}) collective-permute-start(bf16[240,384]{1,0:T(8,128)(2,1)S(1)} %maximum_maximum_fusion), channel_id=1, source_target_pairs={{0,16},{4,20},{8,24},{12,28},{16,0},{20,4},{24,8},{28,12},{1,17},{... | collective-permute-start | bytes 552968 | tf_op jit(solution)/shard_map/ppermute | solution.py:67
  22.7 19.0 %collective-permute-start.14 = (bf16[96,768]{1,0:T(8,128)(2,1)}, bf16[96,768]{1,0:T(8,128)(2,1)S(1)}, u32[]{:S(2)}, u32[]{:S(2)}) collective-permute-start(bf16[96,768]{1,0:T(8,128)(2,1)} %param.15), channel_id=1, source_target_pairs={{0,16},{4,20},{8,24},{12,28},{16,0},{20,4},{24,8},{28,12},{1,17},{... | collective-permute-start | bytes 442376 | tf_op jit(solution)/shard_map/ppermute | solution.py:67
  25.7 17.6 %collective-permute-start.23 = (bf16[240,384]{1,0:T(8,128)(2,1)S(1)}, bf16[240,384]{1,0:T(8,128)(2,1)S(1)}, u32[]{:S(2)}, u32[]{:S(2)}) collective-permute-start(bf16[240,384]{1,0:T(8,128)(2,1)S(1)} %maximum_maximum_fusion), channel_id=1, source_target_pairs={{0,8},{4,12},{8,16},{12,20},{16,24},{20,28},{24,0},{28,4},{1,9},{5... | collective-permute-start | bytes 552968 | tf_op jit(solution)/shard_map/ppermute | solution.py:67
  48.4 20.1 %collective-permute-start.17 = (bf16[4,96,768]{2,1,0:T(8,128)(2,1)S(1)}, bf16[4,96,768]{2,1,0:T(8,128)(2,1)S(1)}, u32[]{:S(2)}, u32[]{:S(2)}) collective-permute-start(bf16[4,96,768]{2,1,0:T(8,128)(2,1)S(1)} %pad_maximum_fusion.1.refs_0_), channel_id=1, source_target_pairs={{0,4},{4,0},{8,12},{12,8},{16,20},{20,16},{24,28},{28,24},{1,5},{5... | collective-permute-start | bytes 1769480 | tf_op jit(solution)/shard_map/ppermute | solution.py:50
  55.8 17.2 %collective-permute-start.29 = (bf16[4,240,384]{2,1,0:T(8,128)(2,1)S(1)}, bf16[4,240,384]{2,1,0:T(8,128)(2,1)}, u32[]{:S(2)}, u32[]{:S(2)}) collective-permute-start(bf16[4,240,384]{2,1,0:T(8,128)(2,1)S(1)} %pad_maximum_fusion.refs_8_), channel_id=1, source_target_pairs={{0,1},{1,0},{2,3},{3,2},{4,5},{5,4},{6,7},{7,6},{8,9},{9,8},{10,11... | collective-permute-start | bytes 2211848 | tf_op jit(solution)/shard_map/ppermute | solution.py:50
  57.7 25.8 %collective-permute-start.27 = (bf16[4,240,384]{2,1,0:T(8,128)(2,1)S(1)}, bf16[4,240,384]{2,1,0:T(8,128)(2,1)}, u32[]{:S(2)}, u32[]{:S(2)}) collective-permute-start(bf16[4,240,384]{2,1,0:T(8,128)(2,1)S(1)} %pad_maximum_fusion.refs_8_), channel_id=1, source_target_pairs={{0,4},{4,0},{8,12},{12,8},{16,20},{20,16},{24,28},{28,24},{1,5},{5... | collective-permute-start | bytes 2211848 | tf_op jit(solution)/shard_map/ppermute | solution.py:50
  68.4 19.0 %collective-permute-start.26 = (bf16[4,240,384]{2,1,0:T(8,128)(2,1)S(1)}, bf16[4,240,384]{2,1,0:T(8,128)(2,1)}, u32[]{:S(2)}, u32[]{:S(2)}) collective-permute-start(bf16[4,240,384]{2,1,0:T(8,128)(2,1)S(1)} %pad_maximum_fusion.refs_8_), channel_id=1, source_target_pairs={{0,2},{1,3},{2,0},{3,1},{4,6},{5,7},{6,4},{7,5},{8,10},{9,11},{10,... | collective-permute-start | bytes 2211848 | tf_op jit(solution)/shard_map/ppermute | solution.py:50
  72.5 90.6 %collective-permute-start = (bf16[1024,768]{1,0:T(8,128)(2,1)S(1)}, bf16[1024,768]{1,0:T(8,128)(2,1)}, u32[]{:S(2)}, u32[]{:S(2)}) collective-permute-start(bf16[1024,768]{1,0:T(8,128)(2,1)S(1)} %bitcast.233), channel_id=1, source_target_pairs={{0,1},{1,0},{2,3},{3,2},{4,5},{5,4},{6,7},{7,6},{8,9},{9,8},{10,11... | collective-permute-start | bytes 4718600 | tf_op jit(solution)/shard_map/ppermute | solution.py:50
  72.5 91.1 %collective-permute-start.2 = (bf16[1024,768]{1,0:T(8,128)(2,1)}, bf16[1024,768]{1,0:T(8,128)(2,1)}, u32[]{:S(2)}, u32[]{:S(2)}) collective-permute-start(bf16[1024,768]{1,0:T(8,128)(2,1)} %collective-permute-done.1.x2_ref), channel_id=1, source_target_pairs={{0,1},{1,0},{2,3},{3,2},{4,5},{5,4},{6,7},{7,6},{8,9},{9,8},{10,11... | collective-permute-start | bytes 4718600 | tf_op jit(solution)/shard_map/ppermute | solution.py:50
  73.0 16.8 %collective-permute-start.11 = (bf16[4,96,576]{2,1,0:T(8,128)(2,1)S(1)}, bf16[4,96,576]{2,1,0:T(8,128)(2,1)S(1)}, u32[]{:S(2)}, u32[]{:S(2)}) collective-permute-start(bf16[4,96,576]{2,1,0:T(8,128)(2,1)S(1)} %collective-permute-done.7.refs_2_), channel_id=1, source_target_pairs={{0,1},{1,0},{2,3},{3,2},{4,5},{5,4},{6,7},{7,6},{8,9},{9,8},{10,11... | collective-permute-start | bytes 1327112 | tf_op jit(solution)/shard_map/ppermute | solution.py:50
  91.4 71.8 %collective-permute-start.28 = (bf16[4,240,384]{2,1,0:T(8,128)(2,1)}, bf16[4,240,384]{2,1,0:T(8,128)(2,1)}, u32[]{:S(2)}, u32[]{:S(2)}) collective-permute-start(bf16[4,240,384]{2,1,0:T(8,128)(2,1)} %collective-permute-done.26.refs_9_), channel_id=1, source_target_pairs={{0,4},{4,0},{8,12},{12,8},{16,20},{20,16},{24,28},{28,24},{1,5},{5... | collective-permute-start | bytes 2211848 | tf_op jit(solution)/shard_map/ppermute | solution.py:50
  101.7 60.9 %collective-permute-start.18 = (bf16[4,96,768]{2,1,0:T(8,128)(2,1)}, bf16[4,96,768]{2,1,0:T(8,128)(2,1)}, u32[]{:S(2)}, u32[]{:S(2)}) collective-permute-start(bf16[4,96,768]{2,1,0:T(8,128)(2,1)} %collective-permute-done.16.refs_1_), channel_id=1, source_target_pairs={{0,4},{4,0},{8,12},{12,8},{16,20},{20,16},{24,28},{28,24},{1,5},{5... | collective-permute-start | bytes 1769480 | tf_op jit(solution)/shard_map/ppermute | solution.py:50
  103.3 59.3 %collective-permute-start.12 = (bf16[4,96,576]{2,1,0:T(8,128)(2,1)}, bf16[4,96,576]{2,1,0:T(8,128)(2,1)}, u32[]{:S(2)}, u32[]{:S(2)}) collective-permute-start(bf16[4,96,576]{2,1,0:T(8,128)(2,1)} %collective-permute-done.8.refs_3_), channel_id=1, source_target_pairs={{0,1},{1,0},{2,3},{3,2},{4,5},{5,4},{6,7},{7,6},{8,9},{9,8},{10,11... | collective-permute-start | bytes 1327112 | tf_op jit(solution)/shard_map/ppermute | solution.py:50
  162.6 55.1 %collective-permute-start.20 = (bf16[4,96,768]{2,1,0:T(8,128)(2,1)}, bf16[4,96,768]{2,1,0:T(8,128)(2,1)S(1)}, u32[]{:S(2)}, u32[]{:S(2)}) collective-permute-start(bf16[4,96,768]{2,1,0:T(8,128)(2,1)} %collective-permute-done.16.refs_1_), channel_id=1, source_target_pairs={{0,1},{1,0},{2,3},{3,2},{4,5},{5,4},{6,7},{7,6},{8,9},{9,8},{10,11... | collective-permute-start | bytes 1769480 | tf_op jit(solution)/shard_map/ppermute | solution.py:50
  162.6 55.0 %collective-permute-start.30 = (bf16[4,240,384]{2,1,0:T(8,128)(2,1)}, bf16[4,240,384]{2,1,0:T(8,128)(2,1)S(1)}, u32[]{:S(2)}, u32[]{:S(2)}) collective-permute-start(bf16[4,240,384]{2,1,0:T(8,128)(2,1)} %collective-permute-done.26.refs_9_), channel_id=1, source_target_pairs={{0,1},{1,0},{2,3},{3,2},{4,5},{5,4},{6,7},{7,6},{8,9},{9,8},{10,11... | collective-permute-start | bytes 2211848 | tf_op jit(solution)/shard_map/ppermute | solution.py:50
  163.1 54.5 %collective-permute-start.31 = (bf16[4,240,384]{2,1,0:T(8,128)(2,1)}, bf16[4,240,384]{2,1,0:T(8,128)(2,1)S(1)}, u32[]{:S(2)}, u32[]{:S(2)}) collective-permute-start(bf16[4,240,384]{2,1,0:T(8,128)(2,1)} %collective-permute-done.27.refs_10_), channel_id=1, source_target_pairs={{0,1},{1,0},{2,3},{3,2},{4,5},{5,4},{6,7},{7,6},{8,9},{9,8},{10,11... | collective-permute-start | bytes 2211848 | tf_op jit(solution)/shard_map/ppermute | solution.py:50
  163.2 55.4 %collective-permute-start.22 = (bf16[4,96,768]{2,1,0:T(8,128)(2,1)}, bf16[4,96,768]{2,1,0:T(8,128)(2,1)S(1)}, u32[]{:S(2)}, u32[]{:S(2)}) collective-permute-start(bf16[4,96,768]{2,1,0:T(8,128)(2,1)} %collective-permute-done.18.refs_3_), channel_id=1, source_target_pairs={{0,1},{1,0},{2,3},{3,2},{4,5},{5,4},{6,7},{7,6},{8,9},{9,8},{10,11... | collective-permute-start | bytes 1769480 | tf_op jit(solution)/shard_map/ppermute | solution.py:50
  163.6 55.8 %collective-permute-start.32 = (bf16[4,240,384]{2,1,0:T(8,128)(2,1)}, bf16[4,240,384]{2,1,0:T(8,128)(2,1)}, u32[]{:S(2)}, u32[]{:S(2)}) collective-permute-start(bf16[4,240,384]{2,1,0:T(8,128)(2,1)} %collective-permute-done.28.refs_11_), channel_id=1, source_target_pairs={{0,1},{1,0},{2,3},{3,2},{4,5},{5,4},{6,7},{7,6},{8,9},{9,8},{10,11... | collective-permute-start | bytes 2211848 | tf_op jit(solution)/shard_map/ppermute | solution.py:50
  302.2 38.5 %collective-permute-start.34 = (bf16[1024,1536]{1,0:T(8,128)(2,1)}, bf16[1024,1536]{1,0:T(8,128)(2,1)S(1)}, u32[]{:S(2)}, u32[]{:S(2)}) collective-permute-start(bf16[1024,1536]{1,0:T(8,128)(2,1)} %bitcast.263), channel_id=1, source_target_pairs={{0,1},{1,0},{2,3},{3,2},{4,5},{5,4},{6,7},{7,6},{8,9},{9,8},{10,11... | collective-permute-start | bytes 9437192 | tf_op jit(solution)/shard_map/ppermute | solution.py:50
  314.1 23.0 %collective-permute-start.42 = (bf16[2,2,4,240,384]{4,3,2,1,0:T(8,128)(2,1)S(1)}, bf16[2,2,4,240,384]{4,3,2,1,0:T(8,128)(2,1)}, u32[]{:S(2)}, u32[]{:S(2)}) collective-permute-start(bf16[2,2,4,240,384]{4,3,2,1,0:T(8,128)(2,1)S(1)} %get-tuple-element.66), channel_id=1, source_target_pairs={{0,1},{1,0},{2,3},{3,2},{4,5},{5,4},{6,7},{7,6},{8,9},{9,8},{10,11... | collective-permute-start | bytes 8847368 | tf_op jit(solution)/shard_map/ppermute | solution.py:50
  325.4 23.6 %collective-permute-start.33 = (bf16[1024,1536]{1,0:T(8,128)(2,1)}, bf16[1024,1536]{1,0:T(8,128)(2,1)S(1)}, u32[]{:S(2)}, u32[]{:S(2)}) collective-permute-start(bf16[1024,1536]{1,0:T(8,128)(2,1)} %bitcast.262), channel_id=1, source_target_pairs={{0,1},{1,0},{2,3},{3,2},{4,5},{5,4},{6,7},{7,6},{8,9},{9,8},{10,11... | collective-permute-start | bytes 9437192 | tf_op jit(solution)/shard_map/ppermute | solution.py:50
  334.9 37.4 %collective-permute-start.49 = (bf16[2,4,96,768]{3,2,1,0:T(8,128)(2,1)}, bf16[2,4,96,768]{3,2,1,0:T(8,128)(2,1)}, u32[]{:S(2)}, u32[]{:S(2)}) collective-permute-start(bf16[2,4,96,768]{3,2,1,0:T(8,128)(2,1)} %fusion.2), channel_id=1, source_target_pairs={{0,4},{4,0},{8,12},{12,8},{16,20},{20,16},{24,28},{28,24},{1,5},{5... | collective-permute-start | bytes 3538952 | tf_op jit(solution)/shard_map/ppermute | solution.py:50
  340.1 56.7 %collective-permute-start.43 = (bf16[2,4,240,384]{3,2,1,0:T(8,128)(2,1)}, bf16[2,4,240,384]{3,2,1,0:T(8,128)(2,1)}, u32[]{:S(2)}, u32[]{:S(2)}) collective-permute-start(bf16[2,4,240,384]{3,2,1,0:T(8,128)(2,1)} %fusion), channel_id=1, source_target_pairs={{0,2},{1,3},{2,0},{3,1},{4,6},{5,7},{6,4},{7,5},{8,10},{9,11},{10,... | collective-permute-start | bytes 4423688 | tf_op jit(solution)/shard_map/ppermute | solution.py:50
  372.2 88.9 %collective-permute-start.36 = (bf16[2,2,4,96,576]{4,3,2,1,0:T(8,128)(2,1)}, bf16[2,2,4,96,576]{4,3,2,1,0:T(8,128)(2,1)}, u32[]{:S(2)}, u32[]{:S(2)}) collective-permute-start(bf16[2,2,4,96,576]{4,3,2,1,0:T(8,128)(2,1)} %get-tuple-element.61), channel_id=1, source_target_pairs={{0,1},{1,0},{2,3},{3,2},{4,5},{5,4},{6,7},{7,6},{8,9},{9,8},{10,11... | collective-permute-start | bytes 5308424 | tf_op jit(solution)/shard_map/ppermute | solution.py:50
  374.8 16.4 %collective-permute-start.50 = (bf16[4,96,768]{2,1,0:T(8,128)(2,1)}, bf16[4,96,768]{2,1,0:T(8,128)(2,1)}, u32[]{:S(2)}, u32[]{:S(2)}) collective-permute-start(bf16[4,96,768]{2,1,0:T(8,128)(2,1)} %fusion.3), channel_id=1, source_target_pairs={{0,2},{1,3},{2,0},{3,1},{4,6},{5,7},{6,4},{7,5},{8,10},{9,11},{10,... | collective-permute-start | bytes 1769480 | tf_op jit(solution)/shard_map/ppermute | solution.py:50
  377.7 93.6 %collective-permute-start.35 = (bf16[1024,768]{1,0:T(8,128)(2,1)}, bf16[1024,768]{1,0:T(8,128)(2,1)}, u32[]{:S(2)}, u32[]{:S(2)}) collective-permute-start(bf16[1024,768]{1,0:T(8,128)(2,1)} %copy-done.18), channel_id=1, source_target_pairs={{0,2},{1,3},{2,0},{3,1},{4,6},{5,7},{6,4},{7,5},{8,10},{9,11},{10,... | collective-permute-start | bytes 4718600 | tf_op jit(solution)/shard_map/ppermute | solution.py:50
  395.2 63.8 %collective-permute-start.53 = (bf16[96,768]{1,0:T(8,128)(2,1)S(1)}, bf16[96,768]{1,0:T(8,128)(2,1)}, u32[]{:S(2)}, u32[]{:S(2)}) collective-permute-start(bf16[96,768]{1,0:T(8,128)(2,1)S(1)} %get-tuple-element.79), channel_id=1, source_target_pairs={{0,24},{4,28},{8,0},{12,4},{16,8},{20,12},{24,16},{28,20},{1,25},{... | collective-permute-start | bytes 442376 | tf_op jit(solution)/shard_map/ppermute | solution.py:67
  396.9 62.1 %collective-permute-start.52 = (bf16[96,768]{1,0:T(8,128)(2,1)S(1)}, bf16[96,768]{1,0:T(8,128)(2,1)}, u32[]{:S(2)}, u32[]{:S(2)}) collective-permute-start(bf16[96,768]{1,0:T(8,128)(2,1)S(1)} %get-tuple-element.80), channel_id=1, source_target_pairs={{0,16},{4,20},{8,24},{12,28},{16,0},{20,4},{24,8},{28,12},{1,17},{... | collective-permute-start | bytes 442376 | tf_op jit(solution)/shard_map/ppermute | solution.py:67
  401.7 63.7 %collective-permute-start.44 = (bf16[4,240,384]{2,1,0:T(8,128)(2,1)}, bf16[4,240,384]{2,1,0:T(8,128)(2,1)}, u32[]{:S(2)}, u32[]{:S(2)}) collective-permute-start(bf16[4,240,384]{2,1,0:T(8,128)(2,1)} %fusion.1), channel_id=1, source_target_pairs={{0,4},{4,0},{8,12},{12,8},{16,20},{20,16},{24,28},{28,24},{1,5},{5... | collective-permute-start | bytes 2211848 | tf_op jit(solution)/shard_map/ppermute | solution.py:50
  463.0 23.3 %collective-permute-start.37 = (bf16[2,4,96,576]{3,2,1,0:T(8,128)(2,1)S(1)}, bf16[2,4,96,576]{3,2,1,0:T(8,128)(2,1)S(1)}, u32[]{:S(2)}, u32[]{:S(2)}) collective-permute-start(bf16[2,4,96,576]{3,2,1,0:T(8,128)(2,1)S(1)} %fusion.4), channel_id=1, source_target_pairs={{0,4},{4,0},{8,12},{12,8},{16,20},{20,16},{24,28},{28,24},{1,5},{5... | collective-permute-start | bytes 2654216 | tf_op jit(solution)/shard_map/ppermute | solution.py:50
  (69 other events, 994.7 us)
